TPU v7x, 256 devices: a whole 4x4x8 slice. The times are simulated.
256 devices in a mesh: dp: 8 (over x, core), ctx: 32 (over z, y).
Axes of the slice: x: 4, y: 4, z: 8, core: 2. Of those that a mesh axis runs over, the one named last changes fastest.
Arguments:
- q_proj: bfloat16 [16384, 4096], P('ctx', 'dp'), may hold values from -6 to 6
- k_proj: bfloat16 [16384, 4096], P('ctx', 'dp'), may hold values from -6 to 6
- v_proj: bfloat16 [16384, 4096], P('ctx', 'dp'), may hold values from -6 to 6
- short_taps: float32 [3, 3, 4096], P(None, None, 'dp'), may hold values from -3 to 3
- long_filter: bfloat16 [16384, 4096], P('ctx', 'dp'), may hold values from -0.046875 to 0.046875
- skip_gain: float32 [4096], P('dp'), may hold values from -4 to 4
- w_out: bfloat16 [4096, 4096], P('dp'), may hold values from -0.125 to 0.125
Outputs:
- layer_out: bfloat16 [16384, 4096], P('ctx', 'dp')
All inputs are finite; a program needn't handle non-finite values.
Results may differ from a plain program's by a relative error of at most 0.006.
Values may be sent and summed in bfloat16 or wider, within the bound.
A program may use at most 128 MiB of HBM per device.

v0:
```python
import math

import jax
import jax.numpy as jnp
from jax import lax
from jax.sharding import PartitionSpec as P

HIGHEST_PRECISION = lax.Precision.HIGHEST


def from_behind(block, axis, distance):
    devices = range(lax.axis_size(axis))
    route = [(i - distance, i) for i in devices if i - distance in devices]
    return lax.ppermute(block, axis, route)


def angle_table(product, period, direction):
    theta = (product % period).astype(jnp.float32) * (2.0 * math.pi / period)
    return (jnp.cos(theta), direction * jnp.sin(theta))


def complex_mul(left_real, left_imag, right_real, right_imag):
    return (
        left_real * right_real - left_imag * right_imag,
        left_real * right_imag + left_imag * right_real,
    )


def complex_dot(form, table, data_real, data_imag):
    table_real, table_imag = table
    if data_imag is None:
        return (
            jnp.einsum(form, table_real, data_real, precision=HIGHEST_PRECISION),
            jnp.einsum(form, table_imag, data_real, precision=HIGHEST_PRECISION),
        )
    out_real = jnp.einsum(form, table_real, data_real, precision=HIGHEST_PRECISION) - jnp.einsum(
        form, table_imag, data_imag, precision=HIGHEST_PRECISION
    )
    out_imag = jnp.einsum(form, table_real, data_imag, precision=HIGHEST_PRECISION) + jnp.einsum(
        form, table_imag, data_real, precision=HIGHEST_PRECISION
    )
    return (out_real, out_imag)


def short_filter(current, previous, filter_taps):
    extended = jnp.concatenate([previous, current], axis=0).astype(jnp.float32)
    return (
        filter_taps[0] * extended[2:]
        + filter_taps[1] * extended[1:-1]
        + filter_taps[2] * extended[:-2]
    )


def conv_positions(mixed_in, kernel, part_count, my_index):
    row_count, channel_count = mixed_in.shape
    per_part = row_count // part_count
    seq_length = row_count * part_count
    fft_total = 2 * seq_length
    arrived = lax.all_to_all(
        jnp.stack([mixed_in, kernel])[:, None], "ctx", split_axis=2, concat_axis=1, tiled=True
    ).astype(jnp.float32)
    frequency = jnp.arange(part_count, dtype=jnp.int32)
    offsets = my_index * per_part + jnp.arange(per_part, dtype=jnp.int32)[None, :]
    location = row_count * frequency[:, None] + offsets
    outer_fwd = angle_table(frequency[:, None] * frequency[None, :], part_count, -1.0)
    turn_fwd = angle_table(frequency[:, None] * offsets, seq_length, -1.0)
    twist_fwd = angle_table(location, fft_total, -1.0)
    gathered_parts = []
    for parity in range(2):
        if parity == 0:
            part_real, part_imag = complex_dot("ka,xajc->xkjc", outer_fwd, arrived, None)
        else:
            part_real, part_imag = complex_dot(
                "ka,xajc->xkjc",
                outer_fwd,
                arrived * twist_fwd[0][:, :, None],
                arrived * twist_fwd[1][:, :, None],
            )
        part_real, part_imag = complex_mul(
            part_real, part_imag, turn_fwd[0][:, :, None], turn_fwd[1][:, :, None]
        )
        gathered_parts += [part_real, part_imag]
    spectra = jnp.stack(gathered_parts, axis=1)
    spectra = lax.all_to_all(spectra, "ctx", split_axis=2, concat_axis=3, tiled=True)[:, :, 0]
    positions = jnp.arange(row_count, dtype=jnp.int32)
    inner_fwd = angle_table(positions[:, None] * positions[None, :], row_count, -1.0)
    spec_real, spec_imag = complex_dot(
        "mj,xejc->xemc", inner_fwd, spectra[:, 0::2], spectra[:, 1::2]
    )
    prod_real, prod_imag = complex_mul(spec_real[0], spec_imag[0], spec_real[1], spec_imag[1])
    inner_back = angle_table(positions[:, None] * positions[None, :], row_count, 1.0)
    back_real, back_imag = complex_dot("jm,emc->ejc", inner_back, prod_real, prod_imag)
    turn_back = angle_table(my_index * positions, seq_length, 1.0)
    back_real, back_imag = complex_mul(
        back_real, back_imag, turn_back[0][None, :, None], turn_back[1][None, :, None]
    )
    returned = jnp.stack([back_real, back_imag], axis=1)[:, :, None]
    returned = lax.all_to_all(returned, "ctx", split_axis=3, concat_axis=2, tiled=True)
    outer_back = angle_table(frequency[:, None] * frequency[None, :], part_count, 1.0)
    sum_real, sum_imag = complex_dot("ak,ekjc->eajc", outer_back, returned[:, 0], returned[:, 1])
    twist_back = angle_table(location, fft_total, 1.0)
    values = (
        sum_real[0]
        + sum_real[1] * twist_back[0][:, :, None]
        - sum_imag[1] * twist_back[1][:, :, None]
    ) / fft_total
    values = values.astype(jnp.bfloat16)
    return lax.all_to_all(values, "ctx", split_axis=0, concat_axis=1, tiled=True).reshape(
        row_count, channel_count
    )


def body(q_proj, k_proj, v_proj, short_taps, long_filter, skip_gain, w_out):
    part_count = lax.axis_size("ctx")
    my_index = lax.axis_index("ctx")
    rim_rows = jnp.stack([q_proj[-2:], k_proj[-2:], v_proj[-2:]])
    previous = from_behind(rim_rows, "ctx", 1)
    queries = short_filter(q_proj, previous[0], short_taps[0])
    key_side = short_filter(k_proj, previous[1], short_taps[1])
    value_side = short_filter(v_proj, previous[2], short_taps[2])
    mixed_in = (key_side * value_side).astype(jnp.bfloat16)
    convolved = conv_positions(mixed_in, long_filter, part_count, my_index)
    gated = (
        queries * (convolved.astype(jnp.float32) + skip_gain * mixed_in.astype(jnp.float32))
    ).astype(jnp.bfloat16)
    summed = lax.psum_scatter(
        lax.dot_general(w_out, gated, (((0,), (1,)), ((), ())), preferred_element_type=jnp.float32),
        "dp",
        scatter_dimension=0,
        tiled=True,
    )
    return summed.T.astype(jnp.bfloat16)


def solution(mesh):
    placed = (
        P("ctx", "dp"),
        P("ctx", "dp"),
        P("ctx", "dp"),
        P(None, None, "dp"),
        P("ctx", "dp"),
        P("dp"),
        P("dp", None),
    )
    return jax.shard_map(
        body, mesh=mesh, in_specs=placed, out_specs=P("ctx", "dp"), check_vma=False
    )
```

profile of v0, /device:TPU:1, one launch (start us, length us, event | category | flops | bytes accessed | tf_op | source)
XLA Modules:
  0.0 612.9 jit_solution(10586031689923739047)
XLA Ops:
  8.0 4.0 collective-permute-start
  16.5 2.1 copy.25
  18.5 12.5 %all-to-all-start = ((bf16[2,1,512,512]{3,0,1,2:T(2,128)(2,1)}), bf16[2,1,512,512]{3,0,1,2:T(2,128)(2,1)S(1)}, u32[]{:S(2)}, u32[]{:S(2)}) async-start(bf16[2,1,512,512]{3,0,1,2:T(2,128)(2,1)} %copy.25), calls=%async_computation | async-start | bytes 2097152 | tf_op jit(solution)/shard_map/all_to_all | solution.py:59
  31.3 24.6 %all-to-all-done = bf16[2,1,512,512]{3,0,1,2:T(2,128)(2,1)S(1)} async-done(((bf16[2,1,512,512]{3,0,1,2:T(2,128)(2,1)}), bf16[2,1,512,512]{3,0,1,2:T(2,128)(2,1)S(1)}, u32[]{:S(2)}, u32[]{:S(2)}) %all-to-all-start) | async-done | bytes 1048608 | tf_op jit(solution)/shard_map/all_to_all | solution.py:59
  56.4 3.3 fusion.32
  59.7 3.4 fusion.34
  66.1 4.1 fusion.43
  70.2 4.7 fusion.25
  76.6 8.1 %copy.35 = f32[2,4,32,16,512]{4,3,0,1,2:T(8,128)} copy(f32[2,4,32,16,512]{4,2,3,0,1:T(8,128)S(1)} %pad_maximum_fusion) | data formatting | bytes 16777216 | tf_op jit(solution)/shard_map/stack | solution.py:83
  84.7 7.2 %all-to-all-start.1 = ((f32[2,4,32,16,512]{4,3,0,1,2:T(8,128)}), f32[2,4,32,16,512]{4,3,0,1,2:T(8,128)}, u32[]{:S(2)}, u32[]{:S(2)}) async-start(f32[2,4,32,16,512]{4,3,0,1,2:T(8,128)} %copy.35), calls=%async_computation.1 | async-start | bytes 16777216 | tf_op jit(solution)/shard_map/all_to_all | solution.py:84
  92.0 179.9 %all-to-all-done.1 = f32[2,4,32,16,512]{4,3,0,1,2:T(8,128)} async-done(((f32[2,4,32,16,512]{4,3,0,1,2:T(8,128)}), f32[2,4,32,16,512]{4,3,0,1,2:T(8,128)}, u32[]{:S(2)}, u32[]{:S(2)}) %all-to-all-start.1) | async-done | bytes 8388640 | tf_op jit(solution)/shard_map/all_to_all | solution.py:84
  271.9 4.4 copy.36
  276.3 18.0 %fusion = f32[2,2,512,512]{3,2,1,0:T(8,128)S(1)} fusion(f32[2,4,512,512]{3,2,1,0:T(8,128)S(1)} %bitcast.204), kind=kOutput, calls=%fused_computation.5 | convolution fusion | flops 6446383104 | bytes 8388608 | tf_op jit(solution)/shard_map/mj,xejc->xemc/dot_general | solution.py:36
  294.3 18.3 %fusion.2 = f32[2,2,512,512]{3,2,1,0:T(8,128)S(1)} fusion(f32[2,4,512,512]{3,2,1,0:T(8,128)S(1)} %bitcast.205), kind=kOutput, calls=%fused_computation.7 | convolution fusion | flops 6446120960 | bytes 8388608 | tf_op jit(solution)/shard_map/mj,xejc->xemc/dot_general | solution.py:39
  312.6 18.3 %subtract_bitcast_fusion = f32[2,2,512,512]{2,3,1,0:T(8,128)S(1)} fusion(f32[2,2,512,512]{3,2,1,0:T(8,128)S(1)} %fusion, f32[2,4,512,512]{3,2,1,0:T(8,128)S(1)} %bitcast.206), kind=kOutput, calls=%fused_computation.4 | convolution fusion | flops 6447169536 | bytes 12582912 | tf_op jit(solution)/shard_map/mj,xejc->xemc/dot_general | solution.py:36
  330.9 18.1 %add_bitcast_fusion = f32[2,2,512,512]{2,3,1,0:T(8,128)S(1)} fusion(f32[2,2,512,512]{3,2,1,0:T(8,128)S(1)} %fusion.2, f32[2,4,512,512]{3,2,1,0:T(8,128)S(1)} %bitcast.207), kind=kOutput, calls=%fused_computation.3 | convolution fusion | flops 6447431680 | bytes 12582912 | tf_op jit(solution)/shard_map/mj,xejc->xemc/dot_general | solution.py:39
  350.3 8.4 %fusion.14 = f32[2,512,512]{2,1,0:T(8,128)S(1)} fusion(f32[1,2,512,512]{2,3,1,0:T(8,128)S(1)} %get-tuple-element.6), kind=kOutput, calls=%fused_computation.19 | convolution fusion | flops 3224895488 | bytes 4194304 | tf_op jit(solution)/shard_map/jm,emc->ejc/dot_general | solution.py:36
  358.7 8.4 %fusion.12 = f32[2,512,512]{2,1,0:T(8,128)S(1)} fusion(f32[1,2,512,512]{2,3,1,0:T(8,128)S(1)} %get-tuple-element.6), kind=kOutput, calls=%fused_computation.17 | convolution fusion | flops 3224895488 | bytes 4194304 | tf_op jit(solution)/shard_map/jm,emc->ejc/dot_general | solution.py:39
  367.1 8.7 %fusion.46 = f32[2,512,512]{2,1,0:T(8,128)S(1)} fusion(f32[2,512,512]{2,1,0:T(8,128)S(1)} %fusion.14, f32[1,2,512,512]{2,3,1,0:T(8,128)S(1)} %get-tuple-element.5), kind=kOutput, calls=%fused_computation.61 | convolution fusion | flops 3225419776 | bytes 6291456 | tf_op jit(solution)/shard_map/jm,emc->ejc/dot_general | solution.py:36
  375.8 8.7 %subtract_bitcast_fusion.2 = (f32[2,1,512,512]{2,3,0,1:T(8,128)S(1)}, f32[2,1,512,512]{2,3,0,1:T(8,128)S(1)}) fusion(f32[2,512,512]{2,1,0:T(8,128)S(1)} %fusion.46, f32[512]{0:T(512)S(1)} %get-tuple-element.38, f32[512]{0:T(512)S(1)} %get-tuple-element.39, f32[2,512,512]{2,1,0:T(8,128)S(1)} %fusion.12, f32[1,2,512,512]{2,3,1,0:T(8,128)S(1)} %get-tuple-element.5), kind=kOutput, calls=%fused_computation.44 | convolution fusion | flops 3228565504 | bytes 10489856 | tf_op jit(solution)/shard_map/jm,emc->ejc/dot_general | solution.py:39
  384.5 2.4 maximum_bitcast_fusion
  386.9 7.3 %copy.39 = f32[2,2,1,512,512]{4,0,1,2,3:T(2,128)} copy(f32[2,2,1,512,512]{3,4,0,1,2:T(8,128)} %maximum_bitcast_fusion) | data formatting | bytes 8388608 | tf_op jit(solution)/shard_map/broadcast_in_dim | solution.py:97
  394.2 108.9 %all_to_all.42 = f32[2,2,1,512,512]{4,0,1,2,3:T(2,128)S(1)} all-to-all(f32[2,2,1,512,512]{4,0,1,2,3:T(2,128)} %copy.39), channel_id=1, replica_groups=mesh['dp'=8,'ctx'=32] {'ctx'}, dimensions={3} | all-to-all | bytes 8388608 | tf_op jit(solution)/shard_map/all_to_all | solution.py:98
  505.3 3.3 fusion.29
  508.7 3.3 fusion.28
  512.0 3.5 subtract_bitcast_fusion.1
  515.5 3.7 add_bitcast_fusion.1
  520.6 6.7 %all-to-all-start.3 = ((bf16[32,16,512]{2,1,0:T(8,128)(2,1)}), bf16[32,16,512]{2,1,0:T(8,128)(2,1)S(1)}, u32[]{:S(2)}, u32[]{:S(2)}) async-start(bf16[32,16,512]{2,1,0:T(8,128)(2,1)} %copy.43), calls=%async_computation.3 | async-start | bytes 1048576 | tf_op jit(solution)/shard_map/all_to_all | solution.py:108
  527.6 14.3 %all-to-all-done.3 = bf16[32,16,512]{2,1,0:T(8,128)(2,1)S(1)} async-done(((bf16[32,16,512]{2,1,0:T(8,128)(2,1)}), bf16[32,16,512]{2,1,0:T(8,128)(2,1)S(1)}, u32[]{:S(2)}, u32[]{:S(2)}) %all-to-all-start.3) | async-done | bytes 524320 | tf_op jit(solution)/shard_map/all_to_all | solution.py:108
  541.9 8.0 %convolution_bitcast_fusion = f32[4096,512]{0,1:T(8,128)} fusion(bf16[512,4096]{1,0:T(8,128)(2,1)} %param.13, f32[514,512]{1,0:T(8,128)S(1)} %maximum_convert_fusion, bf16[512,512]{1,0:T(8,128)(2,1)S(1)} %bitcast.213, bf16[512,512]{1,0:T(8,128)(2,1)S(1)} %fusion.63, f32[512]{0:T(512)S(1)} %copy-done.2, f32[512]{0:T(512)S(1)} %bitcast.216, ...), kind=kOutput, calls=%fused_computation.1 | convolution fusion | flops 2150367232 | bytes 16785408 | tf_op jit(solution)/shard_map/dot_general | solution.py:127
  549.9 53.9 %reduce-scatter.2.cloned.1.call-done = f32[512,512]{0,1:T(8,128)} async-done(((f32[4096,512]{0,1:T(8,128)}), f32[512,512]{0,1:T(8,128)}) %reduce-scatter.2.cloned.1.call-update) | async-done | bytes 1048592 | tf_op jit(solution)/shard_map/reduce_scatter | solution.py:126
  603.8 2.1 convert_bitcast_fusion
  (35 shorter events, 16.3 us)
Async XLA Ops:
  8.0 4.9 collective-permute-start
  15.3 1.0 copy-start.1
  18.5 37.4 %all-to-all-start = ((bf16[2,1,512,512]{3,0,1,2:T(2,128)(2,1)}), bf16[2,1,512,512]{3,0,1,2:T(2,128)(2,1)S(1)}, u32[]{:S(2)}, u32[]{:S(2)}) async-start(bf16[2,1,512,512]{3,0,1,2:T(2,128)(2,1)} %copy.25), calls=%async_computation | async-start | bytes 2097152 | tf_op jit(solution)/shard_map/all_to_all | solution.py:59
  84.7 187.2 %all-to-all-start.1 = ((f32[2,4,32,16,512]{4,3,0,1,2:T(8,128)}), f32[2,4,32,16,512]{4,3,0,1,2:T(8,128)}, u32[]{:S(2)}, u32[]{:S(2)}) async-start(f32[2,4,32,16,512]{4,3,0,1,2:T(8,128)} %copy.35), calls=%async_computation.1 | async-start | bytes 16777216 | tf_op jit(solution)/shard_map/all_to_all | solution.py:84
  519.2 8.1 %copy-start = (bf16[512,512]{1,0:T(8,128)(2,1)S(1)}, bf16[512,512]{1,0:T(8,128)(2,1)}, u32[]{:S(2)}) copy-start(bf16[512,512]{1,0:T(8,128)(2,1)} %param.7) | copy-start | bytes 1572868
  519.5 22.4 %copy-start.2 = (f32[512]{0:T(512)S(1)}, f32[512]{0:T(512)}, u32[]{:S(2)}) copy-start(f32[512]{0:T(512)} %param.12) | copy-start | bytes 6148
  520.6 21.3 %all-to-all-start.3 = ((bf16[32,16,512]{2,1,0:T(8,128)(2,1)}), bf16[32,16,512]{2,1,0:T(8,128)(2,1)S(1)}, u32[]{:S(2)}, u32[]{:S(2)}) async-start(bf16[32,16,512]{2,1,0:T(8,128)(2,1)} %copy.43), calls=%async_computation.3 | async-start | bytes 1048576 | tf_op jit(solution)/shard_map/all_to_all | solution.py:108
  527.3 76.5 %reduce-scatter.2.cloned.1.call-start = ((), (), s32[]{:S(2)}) async-start(), calls=%async_computation.5 | async-start | bytes 9437184 | tf_op jit(solution)/shard_map/reduce_scatter | solution.py:126
Sparse Core Ops, SparseCore 0:
  550.1 53.6 reduce-scatter.1
where the time goes:
time: 617 us; the launch traced here: 613 us
  waiting for transfers between devices  273 us (44%)
  matrix products  147 us (24%)
  blocking collectives  109 us (18%)
  starting transfers between devices  30.4 us (5%)
  local copies, waits for them, and re-layouts  28.2 us (5%)
  between operations  13.9 us (2%)
  other arithmetic  11.5 us (2%)
    all_to_all x1, waiting for transfers between devices, conv_positions(): lax.all_to_all(spectra, 'ctx', split_axis=2, concat_axis=3, tiled=True)  180 us
    all_to_all x1, blocking collectives, conv_positions(): lax.all_to_all(returned, 'ctx', split_axis=3, concat_axis=2, tiled=True)  109 us
    reduce_scatter x1, waiting for transfers between devices, body(): lax.psum_scatter(lax.dot_general(w_out, gated, (((0,), (1,)), ((), ())),...  53.9 us
    dot_general x5, matrix products, complex_dot(): jnp.einsum(form, table_real, data_real, precision=HIGHEST_PRECISION)  36.5 us
    dot_general x5, matrix products, complex_dot(): jnp.einsum(form, table_imag, data_real, precision=HIGHEST_PRECISION)  35.8 us
    dot_general x4, matrix products, complex_dot(): jnp.einsum(form, table_real, data_imag, precision=HIGHEST_PRECISION)  33.7 us
    dot_general x4, matrix products, complex_dot(): jnp.einsum(form, table_imag, data_imag, precision=HIGHEST_PRECISION)  33.3 us
    all_to_all x1, waiting for transfers between devices, conv_positions(): lax.all_to_all(jnp.stack([mixed_in, kernel])[:, None], 'ctx', split_axis=...  24.6 us
  transfers between devices with their start and end apart: 5, of which 4 were waited for; matrix products, arithmetic and copies ran while one was open for 0% of the time, Pallas kernels for 0%

commit v1 on v0

v1 whole, which is shorter than its diff:
```python
import functools
import math

import jax
import jax.numpy as jnp
import ml_dtypes
import numpy as np
from jax import lax
from jax.experimental import pallas as pl
from jax.experimental.pallas import tpu as pltpu
from jax.sharding import PartitionSpec as P

BF16 = jnp.bfloat16
F32 = jnp.float32


def halves(table):
    high = table.astype(ml_dtypes.bfloat16)
    low = (table - high.astype(np.float64)).astype(ml_dtypes.bfloat16)
    return high, low


@functools.lru_cache(None)
def tables(side):
    total = side * side
    index = np.arange(side)
    quarter = index + 0.25
    outer = -2.0 * math.pi * quarter[:, None] * index[None, :] / side
    high, low = halves(np.concatenate([np.cos(outer), np.sin(outer)], axis=0))
    first = np.concatenate([high, low], axis=1)
    turn = -2.0 * math.pi * quarter[:, None] * index[None, :] / total
    twist = np.stack([np.cos(turn), np.sin(turn)]).astype(np.float32)
    inner = -2.0 * math.pi * index[:, None] * index[None, :] / side
    cosine, sine = np.cos(inner), np.sin(inner)
    high, low = halves(np.block([[cosine, sine], [-sine, cosine]]))
    second = np.concatenate([high, high, low], axis=0)
    high, low = halves(np.block([[cosine, -sine], [sine, cosine]]))
    second_back = np.concatenate([high, high, low], axis=0)
    high, low = halves(np.concatenate([np.cos(outer).T, np.sin(outer).T], axis=1) / total)
    first_back = np.concatenate([high, high, low], axis=1)
    return first, twist, second, second_back, first_back


def split(value):
    high = value.astype(BF16)
    low = (value - high.astype(F32)).astype(BF16)
    return high, low


def conv_kernel(x_ref, h_ref, first_ref, twist_ref, second_ref, second_back_ref, first_back_ref, y_ref):
    channels, side, _ = x_ref.shape
    group = 2

    def spectrum(ref, base):
        data = jnp.concatenate([ref[base + i] for i in range(group)], axis=1)
        part = jnp.dot(
            first_ref[...], jnp.concatenate([data, data], axis=0), preferred_element_type=F32
        )
        rows = []
        for i in range(group):
            lanes = slice(i * side, (i + 1) * side)
            real, imag = part[:side, lanes], part[side:, lanes]
            rows.append(
                jnp.concatenate(
                    [
                        real * twist_ref[0] - imag * twist_ref[1],
                        real * twist_ref[1] + imag * twist_ref[0],
                    ],
                    axis=1,
                )
            )
        high, low = split(jnp.concatenate(rows, axis=0))
        return jnp.dot(
            jnp.concatenate([high, low, high], axis=1), second_ref[...], preferred_element_type=F32
        )

    @pl.loop(0, channels // group)
    def _(step):
        base = step * group
        x_spec = spectrum(x_ref, base)
        h_spec = spectrum(h_ref, base)
        x_real, x_imag = x_spec[:, :side], x_spec[:, side:]
        h_real, h_imag = h_spec[:, :side], h_spec[:, side:]
        product = jnp.concatenate(
            [x_real * h_real - x_imag * h_imag, x_real * h_imag + x_imag * h_real], axis=1
        )
        high, low = split(product)
        back = jnp.dot(
            jnp.concatenate([high, low, high], axis=1),
            second_back_ref[...],
            preferred_element_type=F32,
        )
        columns = []
        for i in range(group):
            rows = slice(i * side, (i + 1) * side)
            real, imag = back[rows, :side], back[rows, side:]
            high, low = split(
                jnp.concatenate(
                    [
                        real * twist_ref[0] + imag * twist_ref[1],
                        imag * twist_ref[0] - real * twist_ref[1],
                    ],
                    axis=0,
                )
            )
            columns.append(jnp.concatenate([high, low, high], axis=0))
        values = jnp.dot(
            first_back_ref[...], jnp.concatenate(columns, axis=1), preferred_element_type=F32
        ).astype(BF16)
        for i in range(group):
            y_ref[base + i] = values[:, i * side : (i + 1) * side]


def long_conv(x, h):
    side = x.shape[1]
    return pl.pallas_call(
        conv_kernel,
        out_shape=jax.ShapeDtypeStruct(x.shape, BF16),
        in_specs=[pl.BlockSpec(memory_space=pltpu.VMEM)] * 7,
        out_specs=pl.BlockSpec(memory_space=pltpu.VMEM),
        compiler_params=pltpu.CompilerParams(vmem_limit_bytes=32 * 1024 * 1024),
    )(x, h, *[jnp.asarray(t) for t in tables(side)])


def from_behind(block, axis, distance):
    devices = range(lax.axis_size(axis))
    route = [(i - distance, i) for i in devices if i - distance in devices]
    return lax.ppermute(block, axis, route)


def short_filter(current, previous, filter_taps):
    extended = jnp.concatenate([previous, current], axis=0).astype(F32)
    return (
        filter_taps[0] * extended[2:]
        + filter_taps[1] * extended[1:-1]
        + filter_taps[2] * extended[:-2]
    )


def body(q_proj, k_proj, v_proj, short_taps, long_filter, skip_gain, w_out):
    parts = lax.axis_size("ctx")
    rows, channels = q_proj.shape
    mine = channels // parts
    side = math.isqrt(rows * parts)
    rim_rows = jnp.stack([q_proj[-2:], k_proj[-2:], v_proj[-2:]])
    previous = from_behind(rim_rows, "ctx", 1)
    queries = short_filter(q_proj, previous[0], short_taps[0])
    key_side = short_filter(k_proj, previous[1], short_taps[1])
    value_side = short_filter(v_proj, previous[2], short_taps[2])
    mixed_in = (key_side * value_side).astype(BF16)

    both = jnp.stack([mixed_in.T, long_filter.T]).reshape(2, parts, mine, rows)
    both = both.transpose(1, 0, 2, 3)
    both = lax.all_to_all(both, "ctx", split_axis=0, concat_axis=0, tiled=True)
    both = both.transpose(1, 2, 0, 3).reshape(2, mine, side, side)
    values = long_conv(both[0], both[1])
    values = values.reshape(mine, parts, rows).transpose(1, 0, 2)
    values = lax.all_to_all(values, "ctx", split_axis=0, concat_axis=0, tiled=True)
    convolved = values.reshape(channels, rows).T
    gated = (
        queries * (convolved.astype(F32) + skip_gain * mixed_in.astype(F32))
    ).astype(BF16)
    summed = lax.psum_scatter(
        lax.dot_general(w_out, gated, (((0,), (1,)), ((), ())), preferred_element_type=F32),
        "dp",
        scatter_dimension=0,
        tiled=True,
    )
    return summed.T.astype(BF16)


def solution(mesh):
    placed = (
        P("ctx", "dp"),
        P("ctx", "dp"),
        P("ctx", "dp"),
        P(None, None, "dp"),
        P("ctx", "dp"),
        P("dp"),
        P("dp", None),
    )
    return jax.shard_map(
        body, mesh=mesh, in_specs=placed, out_specs=P("ctx", "dp"), check_vma=False
    )
```

time: 617 us -> 166 us (0.27)
  waiting for transfers between devices: 273 us -> 73.3 us
  matrix products: 147 us -> 8.4 us
  blocking collectives: 109 us -> 38.2 us
  local copies, waits for them, and re-layouts: 28.2 us -> 7.96 us
  starting transfers between devices: 30.4 us -> 10.8 us
  Pallas kernels: 0 us -> 8.67 us
  other arithmetic: 11.5 us -> 5.01 us
    all_to_all x3 -> x1, waiting for transfers between devices: 219 us -> 14 us  [body(): lax.all_to_all(values, 'ctx', split_axis=0, concat_axis=0, tiled=True)]
    dot_general x18 -> x0, matrix products: 139 us -> none  [the longest x5 36.5 us: complex_dot(): jnp.einsum(form, table_real, data_real, precision=HIGHEST_PRECISION)]
    all_to_all x1, blocking collectives: 109 us -> 38.2 us  [body(): both = lax.all_to_all(both, 'ctx', split_axis=0, concat_axis=0, tiled=True)]
    all_to_all x3 -> x1, starting transfers between devices: 26.4 us -> 6.66 us  [body(): lax.all_to_all(values, 'ctx', split_axis=0, concat_axis=0, tiled=True)]
    broadcast_in_dim x2 -> x0, local copies, waits for them, and re-layouts: 9.38 us -> none  [the longest x1 7.31 us: conv_positions(): returned = jnp.stack([back_real, back_imag], axis=1)[:, :, None]]
    pallas_call x0 -> x1, Pallas kernels: none -> 8.67 us  [long_conv(): pl.pallas_call(conv_kernel, out_shape=jax.ShapeDtypeStruct(x.shape, BF16)...]
    another operation x1 -> x0, local copies, waits for them, and re-layouts: 8.09 us -> none  [conv_positions(): spectra = jnp.stack(gathered_parts, axis=1)]
  transfers between devices with their start and end apart: 5 -> 3, of which waited for: 4 -> 3; matrix products, arithmetic and copies ran while one was open for 0% -> 2% of each run, Pallas kernels for 0% -> 0%
where the time goes in v1:
time: 166 us
  waiting for transfers between devices  73.3 us (44%)
  blocking collectives  38.2 us (23%)
  between operations  13.6 us (8%)
  starting transfers between devices  10.8 us (7%)
  Pallas kernels  8.67 us (5%)
  matrix products  8.4 us (5%)
  local copies, waits for them, and re-layouts  7.96 us (5%)
  other arithmetic  5.01 us (3%)
    reduce_scatter x1, waiting for transfers between devices, body(): lax.psum_scatter(lax.dot_general(w_out, gated, (((0,), (1,)), ((), ())),...  54.2 us
    all_to_all x1, blocking collectives, body(): both = lax.all_to_all(both, 'ctx', split_axis=0, concat_axis=0, tiled=True)  38.2 us
    all_to_all x1, waiting for transfers between devices, body(): lax.all_to_all(values, 'ctx', split_axis=0, concat_axis=0, tiled=True)  14 us
    pallas_call x1, Pallas kernels, long_conv(): pl.pallas_call(conv_kernel, out_shape=jax.ShapeDtypeStruct(x.shape, BF16)...  8.67 us
    dot_general x1, matrix products, body(): lax.dot_general(w_out, gated, (((0,), (1,)), ((), ())), preferred_element...  8.4 us
    all_to_all x1, starting transfers between devices, body(): lax.all_to_all(values, 'ctx', split_axis=0, concat_axis=0, tiled=True)  6.66 us
    ppermute x1, waiting for transfers between devices, from_behind(): return lax.ppermute(block, axis, route)  5.15 us
    ppermute x1, starting transfers between devices, from_behind(): return lax.ppermute(block, axis, route)  4.05 us
  transfers between devices with their start and end apart: 3, of which 3 were waited for; matrix products, arithmetic and copies ran while one was open for 2% of the time, Pallas kernels for 0%

profile of v1, /device:TPU:1, one launch (start us, length us, event | category | flops | bytes accessed | tf_op | source)
XLA Modules:
  0.0 165.9 jit_solution(612826269906480641)
XLA Ops:
  6.5 0.8 slice_bitcast_fusion.5
  7.3 0.7 slice_bitcast_fusion.3
  8.1 0.3 copy.26
  8.3 4.1 %collective-permute-start = (bf16[3,2,512]{1,2,0:T(8,128)(2,1)S(1)}, bf16[3,2,512]{1,2,0:T(8,128)(2,1)S(1)}, u32[]{:S(2)}, u32[]{:S(2)}) collective-permute-start(bf16[3,2,512]{1,2,0:T(8,128)(2,1)S(1)} %copy.26), channel_id=1, source_target_pairs={{0,1},{1,2},{2,3},{3,4},{4,5},{5,6},{6,7},{7,8},{8,9},{9,10},{10,1... | collective-permute-start | bytes 18440 | tf_op jit(solution)/shard_map/ppermute | solution.py:128
  12.4 0.9 fusion.17
  13.3 1.3 copy.28
  14.5 0.2 copy.29
  14.8 0.2 copy.30
  15.0 5.1 %collective-permute-done = bf16[3,2,512]{1,2,0:T(8,128)(2,1)S(1)} collective-permute-done((bf16[3,2,512]{1,2,0:T(8,128)(2,1)S(1)}, bf16[3,2,512]{1,2,0:T(8,128)(2,1)S(1)}, u32[]{:S(2)}, u32[]{:S(2)}) %collective-permute-start) | collective-permute-done | bytes 6176 | tf_op jit(solution)/shard_map/ppermute | solution.py:128
  20.2 0.3 maximum_convert_fusion.2
  20.5 0.3 maximum_convert_fusion.1
  20.8 1.9 %fusion.2 = bf16[512,512]{0,1:T(8,128)(2,1)S(1)} fusion(f32[514,512]{0,1:T(8,128)S(1)} %maximum_convert_fusion.2, f32[514,512]{0,1:T(8,128)S(1)} %maximum_convert_fusion.1, f32[512]{0:T(512)S(1)} %bitcast.62, f32[512]{0:T(512)S(1)} %bitcast.63, f32[512]{0:T(512)S(1)} %bitcast.58, f32[512]{0:T(512)S(1)} %bitcast.59, f32[512]{0:T(512)S(1)} %bitcast.60, ...), kind=kLoop, calls=%fused_computation.4 | loop fusion | flops 3145728 | bytes 6828032 | tf_op jit(solution)/shard_map/convert_element_type | solution.py:150
  22.7 0.1 maximum_bitcast_fusion
  22.8 0.1 copy.31
  22.9 38.2 %all_to_all.10 = bf16[32,2,16,512]{3,2,1,0:T(8,128)(2,1)S(1)} all-to-all(bf16[32,2,16,512]{3,2,1,0:T(8,128)(2,1)S(1)} %copy.31), channel_id=1, replica_groups=mesh['dp'=8,'ctx'=32] {'ctx'}, dimensions={0} | all-to-all | bytes 2097152 | tf_op jit(solution)/shard_map/all_to_all | solution.py:154
  61.1 0.1 fusion.16
  61.2 0.3 copy.33
  61.5 0.3 squeeze.22.h_ref
  61.9 0.3 copy.32
  62.2 0.3 squeeze.21.x_ref
  62.5 0.3 copy-done
  62.8 0.1 copy-done.1
  63.1 8.7 %shard_map.118 = bf16[16,128,128]{2,1,0:T(8,128)(2,1)S(1)} custom-call(bf16[16,128,128]{2,1,0:T(8,128)(2,1)S(1)} %squeeze.21.x_ref, bf16[16,128,128]{2,1,0:T(8,128)(2,1)S(1)} %squeeze.22.h_ref, bf16[256,256]{1,0:T(8,128)(2,1)S(1)} %copy-done.4, f32[2,128,128]{2,1,0:T(8,128)S(1)} %copy-done.3, bf16[768,256]{1,0:T(8,128)(2,1)S(1)} %copy-done.1, ...), custom_call_target="tpu_custom_call" | custom-call | tf_op jit(solution)/shard_map/pallas_call | solution.py:116
  71.7 0.3 reshape.35
  72.1 1.1 copy.36
  73.2 6.7 %all-to-all-start.1 = ((bf16[32,16,512]{2,1,0:T(8,128)(2,1)}), bf16[32,16,512]{2,1,0:T(8,128)(2,1)S(1)}, u32[]{:S(2)}, u32[]{:S(2)}) async-start(bf16[32,16,512]{2,1,0:T(8,128)(2,1)} %bitcast.50), calls=%async_computation.1 | async-start | bytes 1048576 | tf_op jit(solution)/shard_map/all_to_all | solution.py:158
  79.9 0.2 copy.27
  80.1 0.3 maximum_convert_fusion
  80.4 14.0 %all-to-all-done.1 = bf16[32,16,512]{2,1,0:T(8,128)(2,1)S(1)} async-done(((bf16[32,16,512]{2,1,0:T(8,128)(2,1)}), bf16[32,16,512]{2,1,0:T(8,128)(2,1)S(1)}, u32[]{:S(2)}, u32[]{:S(2)}) %all-to-all-start.1) | async-done | bytes 524320 | tf_op jit(solution)/shard_map/all_to_all | solution.py:158
  94.4 8.4 %convolution_bitcast_fusion = f32[4096,512]{0,1:T(8,128)} fusion(bf16[512,4096]{1,0:T(8,128)(2,1)} %param.18, f32[514,512]{0,1:T(8,128)S(1)} %maximum_convert_fusion, bf16[512,512]{1,0:T(8,128)(2,1)S(1)} %bitcast.53, bf16[512,512]{0,1:T(8,128)(2,1)S(1)} %fusion.2, f32[512]{0:T(512)S(1)} %copy-done.8, f32[512]{0:T(512)S(1)} %bitcast.56, f32[512]{0:T(512)S(1)} %bitcast.57, ...), kind=kOutput, calls=%fused_computation | convolution fusion | flops 2150367232 | bytes 16785408 | tf_op jit(solution)/shard_map/dot_general | solution.py:164
  102.8 54.2 %reduce-scatter.2.cloned.1.call-done = f32[512,512]{0,1:T(8,128)} async-done(((f32[4096,512]{0,1:T(8,128)}), f32[512,512]{0,1:T(8,128)}) %reduce-scatter.2.cloned.1.call-update) | async-done | bytes 1048592 | tf_op jit(solution)/shard_map/reduce_scatter | solution.py:163
  157.0 2.1 %convert_bitcast_fusion.1 = bf16[512,512]{1,0:T(8,128)(2,1)} fusion(f32[512,512]{0,1:T(8,128)} %reduce-scatter.2.cloned.1.call-done), kind=kLoop, calls=%fused_computation.27 | loop fusion | flops 262144 | bytes 1572864 | tf_op jit(solution)/shard_map/convert_element_type | solution.py:169
  (20 shorter events, 0.3 us)
Async XLA Ops:
  6.5 8.0 %copy-start.5 = (bf16[512,512]{1,0:T(8,128)(2,1)S(1)}, bf16[512,512]{1,0:T(8,128)(2,1)}, u32[]{:S(2)}) copy-start(bf16[512,512]{1,0:T(8,128)(2,1)} %param.14) | copy-start | bytes 1572868
  6.5 8.2 %copy-start.7 = (bf16[512,512]{1,0:T(8,128)(2,1)S(1)}, bf16[512,512]{1,0:T(8,128)(2,1)}, u32[]{:S(2)}) copy-start(bf16[512,512]{1,0:T(8,128)(2,1)} %param.16) | copy-start | bytes 1572868
  8.3 11.8 %collective-permute-start = (bf16[3,2,512]{1,2,0:T(8,128)(2,1)S(1)}, bf16[3,2,512]{1,2,0:T(8,128)(2,1)S(1)}, u32[]{:S(2)}, u32[]{:S(2)}) collective-permute-start(bf16[3,2,512]{1,2,0:T(8,128)(2,1)S(1)} %copy.26), channel_id=1, source_target_pairs={{0,1},{1,2},{2,3},{3,4},{4,5},{5,6},{6,7},{7,8},{8,9},{9,10},{10,1... | collective-permute-start | bytes 18440 | tf_op jit(solution)/shard_map/ppermute | solution.py:128
  61.8 1.0 copy-start
  61.8 1.1 copy-start.1
  61.8 1.1 copy-start.2
  61.8 1.2 copy-start.3
  61.9 1.2 copy-start.4
  72.1 7.8 %copy-start.6 = (bf16[512,512]{1,0:T(8,128)(2,1)S(1)}, bf16[512,512]{1,0:T(8,128)(2,1)}, u32[]{:S(2)}) copy-start(bf16[512,512]{1,0:T(8,128)(2,1)} %param.12) | copy-start | bytes 1572868
  73.2 21.2 %all-to-all-start.1 = ((bf16[32,16,512]{2,1,0:T(8,128)(2,1)}), bf16[32,16,512]{2,1,0:T(8,128)(2,1)S(1)}, u32[]{:S(2)}, u32[]{:S(2)}) async-start(bf16[32,16,512]{2,1,0:T(8,128)(2,1)} %bitcast.50), calls=%async_computation.1 | async-start | bytes 1048576 | tf_op jit(solution)/shard_map/all_to_all | solution.py:158
  79.8 14.6 %copy-start.8 = (f32[512]{0:T(512)S(1)}, f32[512]{0:T(512)}, u32[]{:S(2)}) copy-start(f32[512]{0:T(512)} %param.17) | copy-start | bytes 6148
  79.8 77.2 %reduce-scatter.2.cloned.1.call-start = ((), (), s32[]{:S(2)}) async-start(), calls=%async_computation.3 | async-start | bytes 9437184 | tf_op jit(solution)/shard_map/reduce_scatter | solution.py:163
Sparse Core Ops, SparseCore 0:
  102.9 54.0 reduce-scatter.1

commit v2 on v1

v2 whole, which is shorter than its diff:
```python
import functools
import math

import jax
import jax.numpy as jnp
import ml_dtypes
import numpy as np
from jax import lax
from jax.experimental import pallas as pl
from jax.experimental.pallas import tpu as pltpu
from jax.sharding import PartitionSpec as P

BF16 = jnp.bfloat16
F32 = jnp.float32
MESH = pl.DeviceIdType.MESH

ROWS = 512
CHANNELS = 512
PARTS = 32
CHIPS = 4
SIDE = 128
CUTS = ROWS // SIDE
CHUNK = 8
COLUMNS = 512
HALF = ROWS // 2
STRIP = COLUMNS // 2


def halves(table):
    high = table.astype(ml_dtypes.bfloat16)
    low = (table - high.astype(np.float64)).astype(ml_dtypes.bfloat16)
    return high, low


@functools.lru_cache(None)
def tables(side):
    total = side * side
    index = np.arange(side)
    quarter = index + 0.25
    outer = -2.0 * math.pi * quarter[:, None] * index[None, :] / side
    high, low = halves(np.concatenate([np.cos(outer), np.sin(outer)], axis=0))
    first = np.concatenate([high, low], axis=1)
    turn = -2.0 * math.pi * quarter[:, None] * index[None, :] / total
    twist = np.stack([np.cos(turn), np.sin(turn)]).astype(np.float32)
    inner = -2.0 * math.pi * index[:, None] * index[None, :] / side
    cosine, sine = np.cos(inner), np.sin(inner)
    high, low = halves(np.block([[cosine, sine], [-sine, cosine]]))
    second = np.concatenate([high, high, low], axis=0)
    high, low = halves(np.block([[cosine, -sine], [sine, cosine]]))
    second_back = np.concatenate([high, high, low], axis=0)
    high, low = halves(np.concatenate([np.cos(outer).T, np.sin(outer).T], axis=1) / total)
    first_back = np.concatenate([high, high, low], axis=1)
    return first, twist, second, second_back, first_back


def split(value):
    high = value.astype(BF16)
    low = (value - high.astype(F32)).astype(BF16)
    return high, low


def kernel(
    q_hbm, k_hbm, v_hbm, h_hbm, w_hbm, taps_ref, skip_ref,
    first_hbm, twist_hbm, second_hbm, second_back_hbm, first_back_hbm,
    out_ref,
    q_in, k_in, v_in, h_in, w_all, first, twist, second, second_back, first_back,
    rim, wide_k, wide_v, turned, mixed, queries,
    h_send, h_recv, x_send, x_recv, flat, spectra, y_flat, y_send, y_recv, back,
    gated, far_send, far_recv, near_send, near_recv,
    load_sem, rim_sems, w_load_sem, w_sems, h_sems, x_sems, y_sems, gated_sems, far_sems, near_sems,
):
    me_dp, me = lax.axis_index("dp"), lax.axis_index("ctx")
    chip, core = me_dp // 2, me_dp % 2
    pair = (chip * 2 + 1 - core, me)
    right = (lax.rem(chip + 1, CHIPS) * 2 + core, me)
    left = (lax.rem(chip + CHIPS - 1, CHIPS) * 2 + core, me)

    def partner(step):
        away = jnp.where(step % 2 == 0, step // 2 + 1, PARTS - (step + 1) // 2)
        return lax.rem(me + away, PARTS)

    barrier = pltpu.get_barrier_semaphore()

    @pl.loop(0, PARTS - 1)
    def _(step):
        pl.semaphore_signal(barrier, inc=1, device_id=(me_dp, partner(step)), device_id_type=MESH)

    for other in (pair, right, left):
        pl.semaphore_signal(barrier, inc=1, device_id=other, device_id_type=MESH)

    loads = [
        pltpu.make_async_copy(source, target, load_sem.at[n])
        for n, (source, target) in enumerate(
            [
                (h_hbm, h_in), (k_hbm, k_in), (v_hbm, v_in), (q_hbm, q_in),
                (first_hbm, first), (twist_hbm, twist), (second_hbm, second),
                (second_back_hbm, second_back), (first_back_hbm, first_back),
            ]
        )
    ]
    for load in loads:
        load.start()

    def remote(source, target, sems, n, device):
        return pltpu.make_async_remote_copy(
            src_ref=source, dst_ref=target, send_sem=sems.at[(0, *n)], recv_sem=sems.at[(1, *n)],
            device_id=device, device_id_type=MESH,
        )

    loads[0].wait()

    @pl.loop(0, CUTS)
    def _(cut):
        rows = pl.ds(pl.multiple_of(cut * SIDE, SIDE), SIDE)
        for tile in range(CHANNELS // SIDE):
            lanes = slice(tile * SIDE, (tile + 1) * SIDE)
            turned[cut, lanes, :] = h_in[rows, lanes].astype(F32).T

    pl.semaphore_wait(barrier, PARTS - 1 + 3)

    rims = [
        remote(hbm.at[pl.ds(ROWS - 16, 16)], rim.at[n], rim_sems, (n,), (me_dp, lax.rem(me + 1, PARTS)))
        for n, hbm in enumerate([q_hbm, k_hbm, v_hbm])
    ]
    for copy in rims:
        copy.start()

    def packed(device, chunk):
        rows = pl.ds(pl.multiple_of(device * 2 * CHUNK + chunk * CHUNK, CHUNK), CHUNK)
        return jnp.concatenate([turned[cut, rows, :] for cut in range(CUTS)], axis=0).astype(BF16)

    @pl.loop(0, PARTS - 1)
    def _(step):
        to = partner(step)
        for chunk in range(2):
            h_send[chunk, to] = packed(to, chunk)
        remote(h_send.at[:, to], h_recv.at[:, me], h_sems, (), (me_dp, to)).start()

    for chunk in range(2):
        h_recv[chunk, me] = packed(me, chunk)

    def widen(source, target, stream):
        target[0:8, :] = jnp.where(me > 0, rim[stream].astype(F32)[8:16, :], 0.0)
        target[8 : 8 + ROWS, :] = source[...].astype(F32)

    def short(wide, stream, cut, lanes):
        window = wide[pl.ds(pl.multiple_of(cut * SIDE, SIDE), SIDE + 8), lanes]
        return (
            taps_ref[stream, 0:1, lanes] * window[8:]
            + taps_ref[stream, 1:2, lanes] * window[7:-1]
            + taps_ref[stream, 2:3, lanes] * window[6:-2]
        )

    loads[1].wait()
    loads[2].wait()
    rims[1].wait()
    rims[2].wait()
    widen(k_in, wide_k, 1)
    widen(v_in, wide_v, 2)

    @pl.loop(0, CUTS)
    def _(cut):
        rows = pl.ds(pl.multiple_of(cut * SIDE, SIDE), SIDE)
        for tile in range(CHANNELS // SIDE):
            lanes = slice(tile * SIDE, (tile + 1) * SIDE)
            value = (short(wide_k, 1, cut, lanes) * short(wide_v, 2, cut, lanes)).astype(BF16)
            mixed[rows, lanes] = value
            turned[cut, lanes, :] = value.astype(F32).T

    for chunk in range(2):

        @pl.loop(0, PARTS - 1)
        def _(step, chunk=chunk):
            to = partner(step)
            x_send[chunk, to] = packed(to, chunk)
            remote(x_send.at[chunk, to], x_recv.at[chunk, me], x_sems, (chunk,), (me_dp, to)).start()

        x_recv[chunk, me] = packed(me, chunk)

    def columns(chip_to, core_to):
        return pl.ds(pl.multiple_of((chip_to * 2 + core_to) * COLUMNS, COLUMNS), COLUMNS)

    w_loads = [
        pltpu.make_async_copy(w_hbm.at[:, columns(n, core)], w_all.at[core, n], w_load_sem.at[n])
        for n in range(CHIPS)
    ]
    w_sent = [
        remote(w_hbm.at[:, columns(n, 1 - core)], w_all.at[core, n], w_sems, (n,), pair)
        for n in range(CHIPS)
    ]
    for copy in w_loads + w_sent:
        copy.start()

    loads[3].wait()
    rims[0].wait()
    widen(q_in, wide_k, 0)

    @pl.loop(0, CUTS)
    def _(cut):
        rows = pl.ds(pl.multiple_of(cut * SIDE, SIDE), SIDE)
        for tile in range(CHANNELS // SIDE):
            lanes = slice(tile * SIDE, (tile + 1) * SIDE)
            queries[rows, lanes] = short(wide_k, 0, cut, lanes)

    def spectrum(base):
        data = jnp.concatenate(
            [flat[pl.ds(base + n, SIDE, stride=CHUNK), :] for n in range(2)], axis=1
        ).astype(BF16)
        part = jnp.dot(first[...], jnp.concatenate([data, data], axis=0), preferred_element_type=F32)
        rows = []
        for n in range(2):
            lanes = slice(n * SIDE, (n + 1) * SIDE)
            real, imag = part[:SIDE, lanes], part[SIDE:, lanes]
            rows.append(
                jnp.concatenate(
                    [real * twist[0] - imag * twist[1], real * twist[1] + imag * twist[0]], axis=1
                )
            )
        high, low = split(jnp.concatenate(rows, axis=0))
        return jnp.dot(
            jnp.concatenate([high, low, high], axis=1), second[...], preferred_element_type=F32
        )

    def all_but_one(send, recv, sems, n=()):
        return remote(send, recv, sems, n, (me_dp, lax.rem(me + 1, PARTS)))

    for load in loads[4:]:
        load.wait()
    some = pl.ds(0, PARTS - 1)
    h_all = all_but_one(h_send.at[:, some], h_recv.at[:, some], h_sems)
    h_all.wait_recv()
    for chunk in range(2):

        @pl.loop(0, PARTS)
        def _(source, chunk=chunk):
            rows = pl.ds(pl.multiple_of(source * CUTS * CHUNK, CUTS * CHUNK), CUTS * CHUNK)
            flat[rows, :] = h_recv[chunk, source].astype(F32)

        @pl.loop(0, CHUNK // 2)
        def _(step, chunk=chunk):
            spectra[chunk * (CHUNK // 2) + step] = spectrum(step * 2)

    sent = []
    for chunk in range(2):
        x_all = all_but_one(x_send.at[chunk, some], x_recv.at[chunk, some], x_sems, (chunk,))
        x_all.wait_recv()
        sent.append(x_all)

        @pl.loop(0, PARTS)
        def _(source, chunk=chunk):
            rows = pl.ds(pl.multiple_of(source * CUTS * CHUNK, CUTS * CHUNK), CUTS * CHUNK)
            flat[rows, :] = x_recv[chunk, source].astype(F32)

        @pl.loop(0, CHUNK // 2)
        def _(step, chunk=chunk):
            x_spec = spectrum(step * 2)
            h_spec = spectra[chunk * (CHUNK // 2) + step]
            x_real, x_imag = x_spec[:, :SIDE], x_spec[:, SIDE:]
            h_real, h_imag = h_spec[:, :SIDE], h_spec[:, SIDE:]
            high, low = split(
                jnp.concatenate(
                    [x_real * h_real - x_imag * h_imag, x_real * h_imag + x_imag * h_real], axis=1
                )
            )
            product = jnp.dot(
                jnp.concatenate([high, low, high], axis=1),
                second_back[...],
                preferred_element_type=F32,
            )
            stacked = []
            for n in range(2):
                rows = slice(n * SIDE, (n + 1) * SIDE)
                real, imag = product[rows, :SIDE], product[rows, SIDE:]
                high, low = split(
                    jnp.concatenate(
                        [real * twist[0] + imag * twist[1], imag * twist[0] - real * twist[1]], axis=0
                    )
                )
                stacked.append(jnp.concatenate([high, low, high], axis=0))
            values = jnp.dot(
                first_back[...], jnp.concatenate(stacked, axis=1), preferred_element_type=F32
            )
            for n in range(2):
                y_flat[pl.ds(step * 2 + n, SIDE, stride=CHUNK), :] = values[:, n * SIDE : (n + 1) * SIDE]

        for half in range(2):

            def piece(device, half=half):
                rows = pl.ds(pl.multiple_of(device * CUTS * CHUNK + half * 16, 16), 16)
                return y_flat[rows, :].astype(BF16)

            @pl.loop(0, PARTS - 1)
            def _(step, chunk=chunk, half=half, piece=piece):
                to = partner(step)
                y_send[chunk, half, to] = piece(to)
                remote(
                    y_send.at[chunk, half, to], y_recv.at[chunk, half, me], y_sems, (chunk, half),
                    (me_dp, to),
                ).start()

            y_recv[chunk, half, me] = piece(me)

    def gate(half):
        for chunk in range(2):
            y_all = all_but_one(
                y_send.at[chunk, half, some], y_recv.at[chunk, half, some], y_sems, (chunk, half)
            )
            y_all.wait_recv()
            sent.append(y_all)

        @pl.loop(0, PARTS)
        def _(source):
            for chunk in range(2):
                value = y_recv[chunk, half, source].astype(F32)
                rows = pl.ds(pl.multiple_of(source * 2 * CHUNK + chunk * CHUNK, CHUNK), CHUNK)
                for n in range(2):
                    back[n, rows, :] = value[n * CHUNK : (n + 1) * CHUNK, :]

        @pl.loop(0, 2)
        def _(n):
            rows = pl.ds(pl.multiple_of(half * HALF + n * SIDE, SIDE), SIDE)
            for tile in range(CHANNELS // SIDE):
                lanes = slice(tile * SIDE, (tile + 1) * SIDE)
                convolved = back[n, lanes, :].T
                direct = skip_ref[0:1, lanes] * mixed[rows, lanes].astype(F32)
                gated[core, rows, lanes] = (queries[rows, lanes] * (convolved + direct)).astype(BF16)

        block = gated.at[core, pl.ds(half * HALF, HALF)]
        copy = remote(block, block, gated_sems, (half,), pair)
        copy.start()
        return copy

    def partial(half, to, strip):
        rows, lanes = slice(half * HALF, (half + 1) * HALF), slice(strip * STRIP, (strip + 1) * STRIP)
        return jnp.dot(
            gated[0, rows, :], w_all[0, to, :, lanes], preferred_element_type=F32
        ) + jnp.dot(gated[1, rows, :], w_all[1, to, :, lanes], preferred_element_type=F32)

    chip_right, chip_left = lax.rem(chip + 1, CHIPS), lax.rem(chip + CHIPS - 1, CHIPS)
    chip_across = lax.rem(chip + 2, CHIPS)
    far, near = {}, {}
    ways = ((0, right, chip_right), (1, left, chip_left))
    for half in range(2):
        exchanged = gate(half)
        if half == 0:
            for copy in w_loads + w_sent:
                copy.wait()
        exchanged.wait()
        for way, device, _ in ways:
            far_send[half, way] = partial(half, chip_across, way).astype(BF16)
            far[half, way] = remote(
                far_send.at[half, way], far_recv.at[half, way], far_sems, (half, way), device
            )
            far[half, way].start()
    for half in range(2):
        for way, device, to in ways:
            far[half, way].wait_recv()
            for strip in range(2):
                value = partial(half, to, strip)
                if strip == way:
                    value = value + far_recv[half, way].astype(F32)
                near_send[half, way, :, strip * STRIP : (strip + 1) * STRIP] = value.astype(BF16)
            near[half, way] = remote(
                near_send.at[half, way], near_recv.at[half, way], near_sems, (half, way), device
            )
            near[half, way].start()
    for half in range(2):
        for way in range(2):
            near[half, way].wait_recv()
        rows = slice(half * HALF, (half + 1) * HALF)
        for strip in range(2):
            lanes = slice(strip * STRIP, (strip + 1) * STRIP)
            out_ref[rows, lanes] = (
                partial(half, chip, strip)
                + near_recv[half, 0, :, lanes].astype(F32)
                + near_recv[half, 1, :, lanes].astype(F32)
            ).astype(BF16)

    for copy in [h_all, *sent, *far.values(), *near.values()]:
        copy.wait_send()


def body(q_proj, k_proj, v_proj, short_taps, long_filter, skip_gain, w_out):
    constants = [jnp.asarray(t) for t in tables(SIDE)]
    wide = (8 + ROWS, CHANNELS)
    stream = (ROWS, CHANNELS)
    travel = (2, PARTS, CUTS * CHUNK, SIDE)
    pieces = (2, 2, PARTS, 16, SIDE)
    dma = pltpu.SemaphoreType.DMA
    anywhere = pl.BlockSpec(memory_space=pl.ANY)
    local = pl.BlockSpec(memory_space=pltpu.VMEM)
    return pl.pallas_call(
        kernel,
        out_shape=jax.ShapeDtypeStruct((ROWS, COLUMNS), BF16),
        in_specs=[anywhere] * 5 + [local] * 2 + [anywhere] * 5,
        out_specs=local,
        scratch_shapes=[
            *[pltpu.VMEM(stream, BF16)] * 4,
            pltpu.VMEM((2, CHIPS, CHANNELS, COLUMNS), BF16),
            *[pltpu.VMEM(t.shape, t.dtype) for t in constants],
            pltpu.VMEM((3, 16, CHANNELS), BF16),
            pltpu.VMEM(wide, F32),
            pltpu.VMEM(wide, F32),
            pltpu.VMEM((CUTS, CHANNELS, SIDE), F32),
            pltpu.VMEM(stream, BF16),
            pltpu.VMEM(stream, F32),
            *[pltpu.VMEM(travel, BF16)] * 4,
            pltpu.VMEM((SIDE * CHUNK, SIDE), F32),
            pltpu.VMEM((CHUNK, 2 * SIDE, 2 * SIDE), F32),
            pltpu.VMEM((SIDE * CHUNK, SIDE), F32),
            *[pltpu.VMEM(pieces, BF16)] * 2,
            pltpu.VMEM((2, CHANNELS, SIDE), F32),
            pltpu.VMEM((2, ROWS, CHANNELS), BF16),
            *[pltpu.VMEM((2, 2, HALF, STRIP), BF16)] * 2,
            *[pltpu.VMEM((2, 2, HALF, COLUMNS), BF16)] * 2,
            dma((9,)),
            dma((2, 3)),
            dma((CHIPS,)),
            dma((2, CHIPS)),
            dma((2,)),
            dma((2, 2)),
            dma((2, 2, 2)),
            dma((2, 2)),
            dma((2, 2, 2)),
            dma((2, 2, 2)),
        ],
        compiler_params=pltpu.CompilerParams(
            collective_id=0, has_side_effects=True, vmem_limit_bytes=56 * 1024 * 1024
        ),
    )(
        q_proj, k_proj, v_proj, long_filter, w_out, short_taps, skip_gain[None, :], *constants
    )


def solution(mesh):
    placed = (
        P("ctx", "dp"),
        P("ctx", "dp"),
        P("ctx", "dp"),
        P(None, None, "dp"),
        P("ctx", "dp"),
        P("dp"),
        P("dp", None),
    )
    return jax.shard_map(
        body, mesh=mesh, in_specs=placed, out_specs=P("ctx", "dp"), check_vma=False
    )
```

time: 166 us -> 79.1 us (0.48)
  waiting for transfers between devices: 73.3 us -> 0 us
  Pallas kernels: 8.67 us -> 77 us
  blocking collectives: 38.2 us -> 0 us
  between operations: 13.6 us -> 0.01 us
  starting transfers between devices: 10.8 us -> 0 us
  matrix products: 8.4 us -> 0 us
  local copies, waits for them, and re-layouts: 7.96 us -> 1.87 us
  other arithmetic: 5.01 us -> 0 us
    pallas_call x1, Pallas kernels: 8.67 us -> 77 us  [body(): pl.pallas_call(kernel, out_shape=jax.ShapeDtypeStruct((ROWS, COLUMNS), BF...]
    reduce_scatter x1 -> x0, waiting for transfers between devices: 54.2 us -> none  [body(): lax.psum_scatter(lax.dot_general(w_out, gated, (((0,), (1,)), ((), ())),...]
    all_to_all x1 -> x0, blocking collectives: 38.2 us -> none  [body(): both = lax.all_to_all(both, 'ctx', split_axis=0, concat_axis=0, tiled=True)]
    all_to_all x1 -> x0, waiting for transfers between devices: 14 us -> none  [body(): lax.all_to_all(values, 'ctx', split_axis=0, concat_axis=0, tiled=True)]
    dot_general x1 -> x0, matrix products: 8.4 us -> none  [body(): lax.dot_general(w_out, gated, (((0,), (1,)), ((), ())), preferred_element...]
    all_to_all x1 -> x0, starting transfers between devices: 6.66 us -> none  [body(): lax.all_to_all(values, 'ctx', split_axis=0, concat_axis=0, tiled=True)]
    ppermute x1 -> x0, waiting for transfers between devices: 5.15 us -> none  [from_behind(): return lax.ppermute(block, axis, route)]
    convert_element_type x5 -> x0, other arithmetic: 4.9 us -> none  [the longest x1 2.08 us: body(): return summed.T.astype(BF16)]
  transfers between devices with their start and end apart: 3 -> 0, of which waited for: 3 -> 0; matrix products, arithmetic and copies ran while one was open for 2% -> 0% of each run, Pallas kernels for 0% -> 0%
where the time goes in v2:
time: 79.1 us; the launch traced here: 78.9 us
  Pallas kernels  77 us (97%)
  local copies, waits for them, and re-layouts  1.87 us (2%)
    pallas_call x1, Pallas kernels, body(): pl.pallas_call(kernel, out_shape=jax.ShapeDtypeStruct((ROWS, COLUMNS), BF...  77 us
    unnamed x1, local copies, waits for them, and re-layouts  1.87 us

profile of v2, /device:TPU:1, one launch (start us, length us, event | category | flops | bytes accessed | tf_op | source)
XLA Modules:
  0.0 78.9 jit_solution(3508193918601888254)
XLA Ops:
  0.0 77.0 %shard_map.118 = bf16[512,512]{1,0:T(8,128)(2,1)} custom-call(bf16[512,512]{1,0:T(8,128)(2,1)} %q_hbm.1, bf16[512,512]{1,0:T(8,128)(2,1)} %k_hbm.1, bf16[512,512]{1,0:T(8,128)(2,1)} %v_hbm.1, bf16[512,512]{1,0:T(8,128)(2,1)} %h_hbm.1, bf16[512,4096]{1,0:T(8,128)(2,1)} %w_hbm.1, f32[3,3,512]{2,1,0:T(4,128)} %taps_ref.1, f32[1,512]{1,0:T(1,128)} %bitcast.1, ...), custom_call_target="tpu_custom_call" | custom-call | tf_op jit(solution)/shard_map/pallas_call | solution.py:392
  77.0 1.9 %copy.14 = bf16[512,512]{1,0:T(8,128)(2,1)} copy(bf16[512,512]{1,0:T(8,128)(2,1)} %shard_map.118) | data formatting | bytes 1048576

commit v3 on v2

--- a/solution.py
+++ b/solution.py
@@ -64,7 +64,7 @@
     first_hbm, twist_hbm, second_hbm, second_back_hbm, first_back_hbm,
     out_ref,
     q_in, k_in, v_in, h_in, w_all, first, twist, second, second_back, first_back,
-    rim, wide_k, wide_v, turned, mixed, queries,
+    rim, wide_k, wide_v, turned_h, turned_x, mixed, queries,
     h_send, h_recv, x_send, x_recv, flat, spectra, y_flat, y_send, y_recv, back,
     gated, far_send, far_recv, near_send, near_recv,
     load_sem, rim_sems, w_load_sem, w_sems, h_sems, x_sems, y_sems, gated_sems, far_sems, near_sems,
@@ -83,7 +83,7 @@
 
     @pl.loop(0, PARTS - 1)
     def _(step):
-        pl.semaphore_signal(barrier, inc=1, device_id=(me_dp, partner(step)), device_id_type=MESH)
+        pl.semaphore_signal(barrier, inc=1, device_id=(me_dp, partner(PARTS - 2 - step)), device_id_type=MESH)
 
     for other in (pair, right, left):
         pl.semaphore_signal(barrier, inc=1, device_id=other, device_id_type=MESH)
@@ -114,7 +114,7 @@
         rows = pl.ds(pl.multiple_of(cut * SIDE, SIDE), SIDE)
         for tile in range(CHANNELS // SIDE):
             lanes = slice(tile * SIDE, (tile + 1) * SIDE)
-            turned[cut, lanes, :] = h_in[rows, lanes].astype(F32).T
+            turned_h[cut, lanes, :] = h_in[rows, lanes].astype(F32).T
 
     pl.semaphore_wait(barrier, PARTS - 1 + 3)
 
@@ -125,19 +125,26 @@
     for copy in rims:
         copy.start()
 
-    def packed(device, chunk):
-        rows = pl.ds(pl.multiple_of(device * 2 * CHUNK + chunk * CHUNK, CHUNK), CHUNK)
-        return jnp.concatenate([turned[cut, rows, :] for cut in range(CUTS)], axis=0).astype(BF16)
-
-    @pl.loop(0, PARTS - 1)
-    def _(step):
-        to = partner(step)
-        for chunk in range(2):
-            h_send[chunk, to] = packed(to, chunk)
-        remote(h_send.at[:, to], h_recv.at[:, me], h_sems, (), (me_dp, to)).start()
-
-    for chunk in range(2):
-        h_recv[chunk, me] = packed(me, chunk)
+    def send_chunk(turned, send, recv, sems, chunk):
+        def packed(device):
+            first_row = chunk * PARTS * CHUNK + device * CHUNK
+            rows = pl.ds(pl.multiple_of(first_row, CHUNK), CHUNK)
+            return jnp.concatenate([turned[cut, rows, :] for cut in range(CUTS)], axis=0).astype(BF16)
+
+        @pl.loop(0, PARTS - 1)
+        def _(step):
+            to = partner(step)
+            send[chunk, to] = packed(to)
+            remote(send.at[chunk, to], recv.at[chunk, me], sems, (chunk,), (me_dp, to)).start()
+
+        recv[chunk, me] = packed(me)
+        some = pl.ds(0, PARTS - 1)
+        return remote(
+            send.at[chunk, some], recv.at[chunk, some], sems, (chunk,), (me_dp, lax.rem(me + 1, PARTS))
+        )
+
+    h_all, x_all = {}, {}
+    h_all[0] = send_chunk(turned_h, h_send, h_recv, h_sems, 0)
 
     def widen(source, target, stream):
         target[0:8, :] = jnp.where(me > 0, rim[stream].astype(F32)[8:16, :], 0.0)
@@ -165,17 +172,9 @@
             lanes = slice(tile * SIDE, (tile + 1) * SIDE)
             value = (short(wide_k, 1, cut, lanes) * short(wide_v, 2, cut, lanes)).astype(BF16)
             mixed[rows, lanes] = value
-            turned[cut, lanes, :] = value.astype(F32).T
-
-    for chunk in range(2):
-
-        @pl.loop(0, PARTS - 1)
-        def _(step, chunk=chunk):
-            to = partner(step)
-            x_send[chunk, to] = packed(to, chunk)
-            remote(x_send.at[chunk, to], x_recv.at[chunk, me], x_sems, (chunk,), (me_dp, to)).start()
-
-        x_recv[chunk, me] = packed(me, chunk)
+            turned_x[cut, lanes, :] = value.astype(F32).T
+
+    x_all[0] = send_chunk(turned_x, x_send, x_recv, x_sems, 0)
 
     def columns(chip_to, core_to):
         return pl.ds(pl.multiple_of((chip_to * 2 + core_to) * COLUMNS, COLUMNS), COLUMNS)
@@ -221,38 +220,26 @@
             jnp.concatenate([high, low, high], axis=1), second[...], preferred_element_type=F32
         )
 
-    def all_but_one(send, recv, sems, n=()):
-        return remote(send, recv, sems, n, (me_dp, lax.rem(me + 1, PARTS)))
-
-    for load in loads[4:]:
-        load.wait()
-    some = pl.ds(0, PARTS - 1)
-    h_all = all_but_one(h_send.at[:, some], h_recv.at[:, some], h_sems)
-    h_all.wait_recv()
-    for chunk in range(2):
-
+    def unpack(arrived, chunk):
         @pl.loop(0, PARTS)
-        def _(source, chunk=chunk):
+        def _(source):
             rows = pl.ds(pl.multiple_of(source * CUTS * CHUNK, CUTS * CHUNK), CUTS * CHUNK)
-            flat[rows, :] = h_recv[chunk, source].astype(F32)
+            flat[rows, :] = arrived[chunk, source].astype(F32)
+
+    def filter_spectra(chunk):
+        h_all[chunk].wait_recv()
+        unpack(h_recv, chunk)
 
         @pl.loop(0, CHUNK // 2)
-        def _(step, chunk=chunk):
+        def _(step):
             spectra[chunk * (CHUNK // 2) + step] = spectrum(step * 2)
 
-    sent = []
-    for chunk in range(2):
-        x_all = all_but_one(x_send.at[chunk, some], x_recv.at[chunk, some], x_sems, (chunk,))
-        x_all.wait_recv()
-        sent.append(x_all)
-
-        @pl.loop(0, PARTS)
-        def _(source, chunk=chunk):
-            rows = pl.ds(pl.multiple_of(source * CUTS * CHUNK, CUTS * CHUNK), CUTS * CHUNK)
-            flat[rows, :] = x_recv[chunk, source].astype(F32)
+    def convolve(chunk):
+        x_all[chunk].wait_recv()
+        unpack(x_recv, chunk)
 
         @pl.loop(0, CHUNK // 2)
-        def _(step, chunk=chunk):
+        def _(step):
             x_spec = spectrum(step * 2)
             h_spec = spectra[chunk * (CHUNK // 2) + step]
             x_real, x_imag = x_spec[:, :SIDE], x_spec[:, SIDE:]
@@ -283,50 +270,66 @@
             for n in range(2):
                 y_flat[pl.ds(step * 2 + n, SIDE, stride=CHUNK), :] = values[:, n * SIDE : (n + 1) * SIDE]
 
-        for half in range(2):
-
-            def piece(device, half=half):
-                rows = pl.ds(pl.multiple_of(device * CUTS * CHUNK + half * 16, 16), 16)
-                return y_flat[rows, :].astype(BF16)
-
-            @pl.loop(0, PARTS - 1)
-            def _(step, chunk=chunk, half=half, piece=piece):
-                to = partner(step)
-                y_send[chunk, half, to] = piece(to)
-                remote(
-                    y_send.at[chunk, half, to], y_recv.at[chunk, half, me], y_sems, (chunk, half),
-                    (me_dp, to),
-                ).start()
-
-            y_recv[chunk, half, me] = piece(me)
-
-    def gate(half):
-        for chunk in range(2):
-            y_all = all_but_one(
-                y_send.at[chunk, half, some], y_recv.at[chunk, half, some], y_sems, (chunk, half)
-            )
-            y_all.wait_recv()
-            sent.append(y_all)
+        @pl.loop(0, PARTS)
+        def _(device):
+            rows = pl.ds(pl.multiple_of(device * CUTS * CHUNK, CUTS * CHUNK), CUTS * CHUNK)
+            value = y_flat[rows, :].astype(BF16)
+            for half in range(2):
+                y_send[chunk, half, device] = value[half * 16 : (half + 1) * 16]
+
+    def send_back(chunk, half):
+        @pl.loop(0, PARTS - 1)
+        def _(step):
+            to = partner(step)
+            remote(
+                y_send.at[chunk, half, to], y_recv.at[chunk, half, me], y_sems, (chunk, half),
+                (me_dp, to),
+            ).start()
+
+        y_recv[chunk, half, me] = y_send[chunk, half, me]
+        some = pl.ds(0, PARTS - 1)
+        return remote(
+            y_send.at[chunk, half, some], y_recv.at[chunk, half, some], y_sems, (chunk, half),
+            (me_dp, lax.rem(me + 1, PARTS)),
+        )
+
+    for load in loads[4:]:
+        load.wait()
+    y_all = {}
+    h_all[0].wait_send()
+    h_all[1] = send_chunk(turned_h, h_send, h_recv, h_sems, 1)
+    filter_spectra(0)
+    x_all[0].wait_send()
+    x_all[1] = send_chunk(turned_x, x_send, x_recv, x_sems, 1)
+    convolve(0)
+    y_all[0, 0] = send_back(0, 0)
+    filter_spectra(1)
+    convolve(1)
+    y_all[1, 0] = send_back(1, 0)
+
+    def gate(chunk, half):
+        y_all[chunk, half].wait_recv()
 
         @pl.loop(0, PARTS)
         def _(source):
-            for chunk in range(2):
-                value = y_recv[chunk, half, source].astype(F32)
-                rows = pl.ds(pl.multiple_of(source * 2 * CHUNK + chunk * CHUNK, CHUNK), CHUNK)
-                for n in range(2):
-                    back[n, rows, :] = value[n * CHUNK : (n + 1) * CHUNK, :]
+            value = y_recv[chunk, half, source].astype(F32)
+            rows = pl.ds(pl.multiple_of(source * CHUNK, CHUNK), CHUNK)
+            for n in range(2):
+                back[n, rows, :] = value[n * CHUNK : (n + 1) * CHUNK, :]
 
         @pl.loop(0, 2)
         def _(n):
             rows = pl.ds(pl.multiple_of(half * HALF + n * SIDE, SIDE), SIDE)
-            for tile in range(CHANNELS // SIDE):
-                lanes = slice(tile * SIDE, (tile + 1) * SIDE)
-                convolved = back[n, lanes, :].T
+            for tile in range(PARTS * CHUNK // SIDE):
+                first_lane = chunk * PARTS * CHUNK + tile * SIDE
+                lanes = slice(first_lane, first_lane + SIDE)
+                convolved = back[n, tile * SIDE : (tile + 1) * SIDE, :].T
                 direct = skip_ref[0:1, lanes] * mixed[rows, lanes].astype(F32)
                 gated[core, rows, lanes] = (queries[rows, lanes] * (convolved + direct)).astype(BF16)
 
-        block = gated.at[core, pl.ds(half * HALF, HALF)]
-        copy = remote(block, block, gated_sems, (half,), pair)
+        lanes = pl.ds(chunk * PARTS * CHUNK, PARTS * CHUNK)
+        block = gated.at[core, pl.ds(half * HALF, HALF), lanes]
+        copy = remote(block, block, gated_sems, (chunk, half), pair)
         copy.start()
         return copy
 
@@ -340,43 +343,59 @@
     chip_across = lax.rem(chip + 2, CHIPS)
     far, near = {}, {}
     ways = ((0, right, chip_right), (1, left, chip_left))
-    for half in range(2):
-        exchanged = gate(half)
-        if half == 0:
-            for copy in w_loads + w_sent:
-                copy.wait()
-        exchanged.wait()
+
+    def send_far(half):
         for way, device, _ in ways:
             far_send[half, way] = partial(half, chip_across, way).astype(BF16)
             far[half, way] = remote(
                 far_send.at[half, way], far_recv.at[half, way], far_sems, (half, way), device
             )
             far[half, way].start()
-    for half in range(2):
+
+    def send_near(half, passed):
         for way, device, to in ways:
-            far[half, way].wait_recv()
-            for strip in range(2):
-                value = partial(half, to, strip)
-                if strip == way:
-                    value = value + far_recv[half, way].astype(F32)
-                near_send[half, way, :, strip * STRIP : (strip + 1) * STRIP] = value.astype(BF16)
-            near[half, way] = remote(
-                near_send.at[half, way], near_recv.at[half, way], near_sems, (half, way), device
-            )
-            near[half, way].start()
-    for half in range(2):
-        for way in range(2):
-            near[half, way].wait_recv()
-        rows = slice(half * HALF, (half + 1) * HALF)
+            strip = way if passed else 1 - way
+            value = partial(half, to, strip)
+            if passed:
+                far[half, way].wait_recv()
+                value = value + far_recv[half, way].astype(F32)
+            near_send[half, way, strip] = value.astype(BF16)
+            near[half, way, strip] = remote(
+                near_send.at[half, way, strip], near_recv.at[half, way, strip], near_sems,
+                (half, way, strip), device,
+            )
+            near[half, way, strip].start()
+
+    def finish(half):
         for strip in range(2):
-            lanes = slice(strip * STRIP, (strip + 1) * STRIP)
-            out_ref[rows, lanes] = (
-                partial(half, chip, strip)
-                + near_recv[half, 0, :, lanes].astype(F32)
-                + near_recv[half, 1, :, lanes].astype(F32)
-            ).astype(BF16)
-
-    for copy in [h_all, *sent, *far.values(), *near.values()]:
+            value = partial(half, chip, strip)
+            for way in range(2):
+                near[half, way, strip].wait_recv()
+                value = value + near_recv[half, way, strip].astype(F32)
+            out_ref[half * HALF : (half + 1) * HALF, strip * STRIP : (strip + 1) * STRIP] = value.astype(BF16)
+
+    exchanged = [gate(0, 0)]
+    y_all[1, 0].wait_send()
+    y_all[0, 1] = send_back(0, 1)
+    y_all[1, 1] = send_back(1, 1)
+    exchanged.append(gate(1, 0))
+    for copy in w_loads + w_sent + exchanged:
+        copy.wait()
+    send_far(0)
+    send_near(0, False)
+    exchanged = [gate(0, 1)]
+    send_near(0, True)
+    exchanged.append(gate(1, 1))
+    for copy in exchanged:
+        copy.wait()
+    send_far(1)
+    send_near(1, False)
+    finish(0)
+    send_near(1, True)
+    finish(1)
+
+    y_all[0, 0].wait_send()
+    for copy in [h_all[1], x_all[1], y_all[0, 1], y_all[1, 1], *far.values(), *near.values()]:
         copy.wait_send()
 
 
@@ -401,7 +420,7 @@
             pltpu.VMEM((3, 16, CHANNELS), BF16),
             pltpu.VMEM(wide, F32),
             pltpu.VMEM(wide, F32),
-            pltpu.VMEM((CUTS, CHANNELS, SIDE), F32),
+            *[pltpu.VMEM((CUTS, CHANNELS, SIDE), F32)] * 2,
             pltpu.VMEM(stream, BF16),
             pltpu.VMEM(stream, F32),
             *[pltpu.VMEM(travel, BF16)] * 4,
@@ -409,20 +428,20 @@
             pltpu.VMEM((CHUNK, 2 * SIDE, 2 * SIDE), F32),
             pltpu.VMEM((SIDE * CHUNK, SIDE), F32),
             *[pltpu.VMEM(pieces, BF16)] * 2,
-            pltpu.VMEM((2, CHANNELS, SIDE), F32),
+            pltpu.VMEM((2, PARTS * CHUNK, SIDE), F32),
             pltpu.VMEM((2, ROWS, CHANNELS), BF16),
             *[pltpu.VMEM((2, 2, HALF, STRIP), BF16)] * 2,
-            *[pltpu.VMEM((2, 2, HALF, COLUMNS), BF16)] * 2,
+            *[pltpu.VMEM((2, 2, 2, HALF, STRIP), BF16)] * 2,
             dma((9,)),
             dma((2, 3)),
             dma((CHIPS,)),
             dma((2, CHIPS)),
-            dma((2,)),
             dma((2, 2)),
-            dma((2, 2, 2)),
             dma((2, 2)),
             dma((2, 2, 2)),
             dma((2, 2, 2)),
+            dma((2, 2, 2)),
+            dma((2, 2, 2, 2)),
         ],
         compiler_params=pltpu.CompilerParams(
             collective_id=0, has_side_effects=True, vmem_limit_bytes=56 * 1024 * 1024

time: 79.1 us -> 77.8 us (0.984)
  Pallas kernels: 77 us -> 75.7 us
    pallas_call x1, Pallas kernels: 77 us -> 75.7 us  [body(): pl.pallas_call(kernel, out_shape=jax.ShapeDtypeStruct((ROWS, COLUMNS), BF...]
where the time goes in v3:
time: 77.8 us; the launch traced here: 77.6 us
  Pallas kernels  75.7 us (97%)
  local copies, waits for them, and re-layouts  1.87 us (2%)
    pallas_call x1, Pallas kernels, body(): pl.pallas_call(kernel, out_shape=jax.ShapeDtypeStruct((ROWS, COLUMNS), BF...  75.7 us
    unnamed x1, local copies, waits for them, and re-layouts  1.87 us

profile of v3, /device:TPU:1, one launch (start us, length us, event | category | flops | bytes accessed | tf_op | source)
XLA Modules:
  0.0 77.6 jit_solution(14904744831142364577)
XLA Ops:
  0.0 75.7 %shard_map.118 = bf16[512,512]{1,0:T(8,128)(2,1)} custom-call(bf16[512,512]{1,0:T(8,128)(2,1)} %q_hbm.1, bf16[512,512]{1,0:T(8,128)(2,1)} %k_hbm.1, bf16[512,512]{1,0:T(8,128)(2,1)} %v_hbm.1, bf16[512,512]{1,0:T(8,128)(2,1)} %h_hbm.1, bf16[512,4096]{1,0:T(8,128)(2,1)} %w_hbm.1, f32[3,3,512]{2,1,0:T(4,128)} %taps_ref.1, f32[1,512]{1,0:T(1,128)} %bitcast.1, ...), custom_call_target="tpu_custom_call" | custom-call | tf_op jit(solution)/shard_map/pallas_call | solution.py:411
  75.7 1.9 %copy.14 = bf16[512,512]{1,0:T(8,128)(2,1)} copy(bf16[512,512]{1,0:T(8,128)(2,1)} %shard_map.118) | data formatting | bytes 1048576

commit v4 on v3

--- a/solution.py
+++ b/solution.py
@@ -75,7 +75,8 @@
     right = (lax.rem(chip + 1, CHIPS) * 2 + core, me)
     left = (lax.rem(chip + CHIPS - 1, CHIPS) * 2 + core, me)
 
-    def partner(step):
+    def partner(turn):
+        step = PARTS - 2 - turn
         away = jnp.where(step % 2 == 0, step // 2 + 1, PARTS - (step + 1) // 2)
         return lax.rem(me + away, PARTS)
 
@@ -83,7 +84,7 @@
 
     @pl.loop(0, PARTS - 1)
     def _(step):
-        pl.semaphore_signal(barrier, inc=1, device_id=(me_dp, partner(PARTS - 2 - step)), device_id_type=MESH)
+        pl.semaphore_signal(barrier, inc=1, device_id=(me_dp, partner(step)), device_id_type=MESH)
 
     for other in (pair, right, left):
         pl.semaphore_signal(barrier, inc=1, device_id=other, device_id_type=MESH)
@@ -230,17 +231,14 @@
         h_all[chunk].wait_recv()
         unpack(h_recv, chunk)
 
-        @pl.loop(0, CHUNK // 2)
-        def _(step):
+        for step in range(CHUNK // 2):
             spectra[chunk * (CHUNK // 2) + step] = spectrum(step * 2)
 
     def convolve(chunk):
         x_all[chunk].wait_recv()
         unpack(x_recv, chunk)
 
-        @pl.loop(0, CHUNK // 2)
-        def _(step):
-            x_spec = spectrum(step * 2)
+        def invert(x_spec, step):
             h_spec = spectra[chunk * (CHUNK // 2) + step]
             x_real, x_imag = x_spec[:, :SIDE], x_spec[:, SIDE:]
             h_real, h_imag = h_spec[:, :SIDE], h_spec[:, SIDE:]
@@ -269,6 +267,12 @@
             )
             for n in range(2):
                 y_flat[pl.ds(step * 2 + n, SIDE, stride=CHUNK), :] = values[:, n * SIDE : (n + 1) * SIDE]
+
+        x_spec = spectrum(0)
+        for step in range(CHUNK // 2):
+            later = spectrum(step * 2 + 2) if step + 1 < CHUNK // 2 else None
+            invert(x_spec, step)
+            x_spec = later
 
         @pl.loop(0, PARTS)
         def _(device):

time: 77.8 us -> 74.3 us (0.955)
  Pallas kernels: 75.7 us -> 72.3 us
    pallas_call x1, Pallas kernels: 75.7 us -> 72.3 us  [body(): pl.pallas_call(kernel, out_shape=jax.ShapeDtypeStruct((ROWS, COLUMNS), BF...]
where the time goes in v4:
time: 74.3 us; the launch traced here: 74.1 us
  Pallas kernels  72.3 us (97%)
  local copies, waits for them, and re-layouts  1.87 us (3%)
    pallas_call x1, Pallas kernels, body(): pl.pallas_call(kernel, out_shape=jax.ShapeDtypeStruct((ROWS, COLUMNS), BF...  72.3 us
    unnamed x1, local copies, waits for them, and re-layouts  1.87 us

profile of v4, /device:TPU:1, one launch (start us, length us, event | category | flops | bytes accessed | tf_op | source)
XLA Modules:
  0.0 74.1 jit_solution(2684806986394257281)
XLA Ops:
  0.0 72.3 %shard_map.118 = bf16[512,512]{1,0:T(8,128)(2,1)} custom-call(bf16[512,512]{1,0:T(8,128)(2,1)} %q_hbm.1, bf16[512,512]{1,0:T(8,128)(2,1)} %k_hbm.1, bf16[512,512]{1,0:T(8,128)(2,1)} %v_hbm.1, bf16[512,512]{1,0:T(8,128)(2,1)} %h_hbm.1, bf16[512,4096]{1,0:T(8,128)(2,1)} %w_hbm.1, f32[3,3,512]{2,1,0:T(4,128)} %taps_ref.1, f32[1,512]{1,0:T(1,128)} %bitcast.1, ...), custom_call_target="tpu_custom_call" | custom-call | tf_op jit(solution)/shard_map/pallas_call | solution.py:415
  72.3 1.9 %copy.14 = bf16[512,512]{1,0:T(8,128)(2,1)} copy(bf16[512,512]{1,0:T(8,128)(2,1)} %shard_map.118) | data formatting | bytes 1048576

commit v5 on v4

--- a/solution.py
+++ b/solution.py
@@ -387,15 +387,14 @@
         copy.wait()
     send_far(0)
     send_near(0, False)
-    exchanged = [gate(0, 1)]
-    send_near(0, True)
-    exchanged.append(gate(1, 1))
+    exchanged = [gate(0, 1), gate(1, 1)]
     for copy in exchanged:
         copy.wait()
     send_far(1)
+    send_near(0, True)
     send_near(1, False)
+    send_near(1, True)
     finish(0)
-    send_near(1, True)
     finish(1)
 
     y_all[0, 0].wait_send()

time: 74.3 us -> 74.3 us (level)
  no operation moved by 1% of the time
where the time goes in v5:
time: 74.3 us; the launch traced here: 74.1 us
  Pallas kernels  72.3 us (97%)
  local copies, waits for them, and re-layouts  1.87 us (3%)
    pallas_call x1, Pallas kernels, body(): pl.pallas_call(kernel, out_shape=jax.ShapeDtypeStruct((ROWS, COLUMNS), BF...  72.3 us
    unnamed x1, local copies, waits for them, and re-layouts  1.87 us

profile of v5, /device:TPU:1, one launch (start us, length us, event | category | flops | bytes accessed | tf_op | source)
XLA Modules:
  0.0 74.1 jit_solution(10183531273961555603)
XLA Ops:
  0.0 72.3 %shard_map.118 = bf16[512,512]{1,0:T(8,128)(2,1)} custom-call(bf16[512,512]{1,0:T(8,128)(2,1)} %q_hbm.1, bf16[512,512]{1,0:T(8,128)(2,1)} %k_hbm.1, bf16[512,512]{1,0:T(8,128)(2,1)} %v_hbm.1, bf16[512,512]{1,0:T(8,128)(2,1)} %h_hbm.1, bf16[512,4096]{1,0:T(8,128)(2,1)} %w_hbm.1, f32[3,3,512]{2,1,0:T(4,128)} %taps_ref.1, f32[1,512]{1,0:T(1,128)} %bitcast.1, ...), custom_call_target="tpu_custom_call" | custom-call | tf_op jit(solution)/shard_map/pallas_call | solution.py:414
  72.3 1.9 %copy.14 = bf16[512,512]{1,0:T(8,128)(2,1)} copy(bf16[512,512]{1,0:T(8,128)(2,1)} %shard_map.118) | data formatting | bytes 1048576

commit v6 on v5

--- a/solution.py
+++ b/solution.py
@@ -64,7 +64,7 @@
     first_hbm, twist_hbm, second_hbm, second_back_hbm, first_back_hbm,
     out_ref,
     q_in, k_in, v_in, h_in, w_all, first, twist, second, second_back, first_back,
-    rim, wide_k, wide_v, turned_h, turned_x, mixed, queries,
+    rim, wide_k, wide_v, wide_q, turned_h, turned_x, mixed, queries,
     h_send, h_recv, x_send, x_recv, flat, spectra, y_flat, y_send, y_recv, back,
     gated, far_send, far_recv, near_send, near_recv,
     load_sem, rim_sems, w_load_sem, w_sems, h_sems, x_sems, y_sems, gated_sems, far_sems, near_sems,
@@ -117,6 +117,56 @@
             lanes = slice(tile * SIDE, (tile + 1) * SIDE)
             turned_h[cut, lanes, :] = h_in[rows, lanes].astype(F32).T
 
+    def packed(turned, chunk, device):
+        rows = pl.ds(pl.multiple_of(chunk * PARTS * CHUNK + device * CHUNK, CHUNK), CHUNK)
+        return jnp.concatenate([turned[cut, rows, :] for cut in range(CUTS)], axis=0).astype(BF16)
+
+    @pl.loop(0, PARTS)
+    def _(device):
+        for chunk in range(2):
+            h_send[chunk, device] = packed(turned_h, chunk, device)
+
+    for chunk in range(2):
+        h_recv[chunk, me] = h_send[chunk, me]
+
+    def widen(source, target):
+        target[8 : 8 + ROWS, :] = source[...].astype(F32)
+
+    def arrive(stream, target):
+        target[0:8, :] = jnp.where(me > 0, rim[stream].astype(F32)[8:16, :], 0.0)
+
+    def short(wide, stream, cut, lanes):
+        window = wide[pl.ds(pl.multiple_of(cut * SIDE, SIDE), SIDE + 8), lanes]
+        return (
+            taps_ref[stream, 0:1, lanes] * window[8:]
+            + taps_ref[stream, 1:2, lanes] * window[7:-1]
+            + taps_ref[stream, 2:3, lanes] * window[6:-2]
+        )
+
+    def mix(first_cut, last_cut):
+        @pl.loop(first_cut, last_cut)
+        def _(cut):
+            rows = pl.ds(pl.multiple_of(cut * SIDE, SIDE), SIDE)
+            for tile in range(CHANNELS // SIDE):
+                lanes = slice(tile * SIDE, (tile + 1) * SIDE)
+                value = (short(wide_k, 1, cut, lanes) * short(wide_v, 2, cut, lanes)).astype(BF16)
+                mixed[rows, lanes] = value
+                turned_x[cut, lanes, :] = value.astype(F32).T
+
+    def query(first_cut, last_cut):
+        @pl.loop(first_cut, last_cut)
+        def _(cut):
+            rows = pl.ds(pl.multiple_of(cut * SIDE, SIDE), SIDE)
+            for tile in range(CHANNELS // SIDE):
+                lanes = slice(tile * SIDE, (tile + 1) * SIDE)
+                queries[rows, lanes] = short(wide_q, 0, cut, lanes)
+
+    for load, source, target in zip(loads[1:4], (k_in, v_in, q_in), (wide_k, wide_v, wide_q)):
+        load.wait()
+        widen(source, target)
+    mix(1, CUTS)
+    query(1, CUTS)
+
     pl.semaphore_wait(barrier, PARTS - 1 + 3)
 
     rims = [
@@ -126,56 +176,38 @@
     for copy in rims:
         copy.start()
 
-    def send_chunk(turned, send, recv, sems, chunk):
-        def packed(device):
-            first_row = chunk * PARTS * CHUNK + device * CHUNK
-            rows = pl.ds(pl.multiple_of(first_row, CHUNK), CHUNK)
-            return jnp.concatenate([turned[cut, rows, :] for cut in range(CUTS)], axis=0).astype(BF16)
-
+    def everyone(send, recv, sems, chunk):
+        some = pl.ds(0, PARTS - 1)
+        return remote(
+            send.at[chunk, some], recv.at[chunk, some], sems, (chunk,), (me_dp, lax.rem(me + 1, PARTS))
+        )
+
+    def send_filter(chunk):
         @pl.loop(0, PARTS - 1)
         def _(step):
             to = partner(step)
-            send[chunk, to] = packed(to)
-            remote(send.at[chunk, to], recv.at[chunk, me], sems, (chunk,), (me_dp, to)).start()
-
-        recv[chunk, me] = packed(me)
-        some = pl.ds(0, PARTS - 1)
-        return remote(
-            send.at[chunk, some], recv.at[chunk, some], sems, (chunk,), (me_dp, lax.rem(me + 1, PARTS))
-        )
+            remote(h_send.at[chunk, to], h_recv.at[chunk, me], h_sems, (chunk,), (me_dp, to)).start()
+
+        return everyone(h_send, h_recv, h_sems, chunk)
+
+    def send_mixed(chunk):
+        @pl.loop(0, PARTS - 1)
+        def _(step):
+            to = partner(step)
+            x_send[chunk, to] = packed(turned_x, chunk, to)
+            remote(x_send.at[chunk, to], x_recv.at[chunk, me], x_sems, (chunk,), (me_dp, to)).start()
+
+        x_recv[chunk, me] = packed(turned_x, chunk, me)
+        return everyone(x_send, x_recv, x_sems, chunk)
 
     h_all, x_all = {}, {}
-    h_all[0] = send_chunk(turned_h, h_send, h_recv, h_sems, 0)
-
-    def widen(source, target, stream):
-        target[0:8, :] = jnp.where(me > 0, rim[stream].astype(F32)[8:16, :], 0.0)
-        target[8 : 8 + ROWS, :] = source[...].astype(F32)
-
-    def short(wide, stream, cut, lanes):
-        window = wide[pl.ds(pl.multiple_of(cut * SIDE, SIDE), SIDE + 8), lanes]
-        return (
-            taps_ref[stream, 0:1, lanes] * window[8:]
-            + taps_ref[stream, 1:2, lanes] * window[7:-1]
-            + taps_ref[stream, 2:3, lanes] * window[6:-2]
-        )
-
-    loads[1].wait()
-    loads[2].wait()
+    h_all[0] = send_filter(0)
     rims[1].wait()
     rims[2].wait()
-    widen(k_in, wide_k, 1)
-    widen(v_in, wide_v, 2)
-
-    @pl.loop(0, CUTS)
-    def _(cut):
-        rows = pl.ds(pl.multiple_of(cut * SIDE, SIDE), SIDE)
-        for tile in range(CHANNELS // SIDE):
-            lanes = slice(tile * SIDE, (tile + 1) * SIDE)
-            value = (short(wide_k, 1, cut, lanes) * short(wide_v, 2, cut, lanes)).astype(BF16)
-            mixed[rows, lanes] = value
-            turned_x[cut, lanes, :] = value.astype(F32).T
-
-    x_all[0] = send_chunk(turned_x, x_send, x_recv, x_sems, 0)
+    arrive(1, wide_k)
+    arrive(2, wide_v)
+    mix(0, 1)
+    x_all[0] = send_mixed(0)
 
     def columns(chip_to, core_to):
         return pl.ds(pl.multiple_of((chip_to * 2 + core_to) * COLUMNS, COLUMNS), COLUMNS)
@@ -190,17 +222,6 @@
     ]
     for copy in w_loads + w_sent:
         copy.start()
-
-    loads[3].wait()
-    rims[0].wait()
-    widen(q_in, wide_k, 0)
-
-    @pl.loop(0, CUTS)
-    def _(cut):
-        rows = pl.ds(pl.multiple_of(cut * SIDE, SIDE), SIDE)
-        for tile in range(CHANNELS // SIDE):
-            lanes = slice(tile * SIDE, (tile + 1) * SIDE)
-            queries[rows, lanes] = short(wide_k, 0, cut, lanes)
 
     def spectrum(base):
         data = jnp.concatenate(
@@ -301,10 +322,10 @@
         load.wait()
     y_all = {}
     h_all[0].wait_send()
-    h_all[1] = send_chunk(turned_h, h_send, h_recv, h_sems, 1)
+    h_all[1] = send_filter(1)
     filter_spectra(0)
     x_all[0].wait_send()
-    x_all[1] = send_chunk(turned_x, x_send, x_recv, x_sems, 1)
+    x_all[1] = send_mixed(1)
     convolve(0)
     y_all[0, 0] = send_back(0, 0)
     filter_spectra(1)
@@ -378,6 +399,9 @@
                 value = value + near_recv[half, way, strip].astype(F32)
             out_ref[half * HALF : (half + 1) * HALF, strip * STRIP : (strip + 1) * STRIP] = value.astype(BF16)
 
+    rims[0].wait()
+    arrive(0, wide_q)
+    query(0, 1)
     exchanged = [gate(0, 0)]
     y_all[1, 0].wait_send()
     y_all[0, 1] = send_back(0, 1)
@@ -421,8 +445,7 @@
             pltpu.VMEM((2, CHIPS, CHANNELS, COLUMNS), BF16),
             *[pltpu.VMEM(t.shape, t.dtype) for t in constants],
             pltpu.VMEM((3, 16, CHANNELS), BF16),
-            pltpu.VMEM(wide, F32),
-            pltpu.VMEM(wide, F32),
+            *[pltpu.VMEM(wide, F32)] * 3,
             *[pltpu.VMEM((CUTS, CHANNELS, SIDE), F32)] * 2,
             pltpu.VMEM(stream, BF16),
             pltpu.VMEM(stream, F32),

time: 74.3 us -> 74 us (level)
  no operation moved by 1% of the time
where the time goes in v6:
time: 74 us; the launch traced here: 73.9 us
  Pallas kernels  72 us (97%)
  local copies, waits for them, and re-layouts  1.87 us (3%)
    pallas_call x1, Pallas kernels, body(): pl.pallas_call(kernel, out_shape=jax.ShapeDtypeStruct((ROWS, COLUMNS), BF...  72 us
    unnamed x1, local copies, waits for them, and re-layouts  1.87 us

profile of v6, /device:TPU:1, one launch (start us, length us, event | category | flops | bytes accessed | tf_op | source)
XLA Modules:
  0.0 73.9 jit_solution(2122567397966757248)
XLA Ops:
  0.0 72.0 %shard_map.118 = bf16[512,512]{1,0:T(8,128)(2,1)} custom-call(bf16[512,512]{1,0:T(8,128)(2,1)} %q_hbm.1, bf16[512,512]{1,0:T(8,128)(2,1)} %k_hbm.1, bf16[512,512]{1,0:T(8,128)(2,1)} %v_hbm.1, bf16[512,512]{1,0:T(8,128)(2,1)} %h_hbm.1, bf16[512,4096]{1,0:T(8,128)(2,1)} %w_hbm.1, f32[3,3,512]{2,1,0:T(4,128)} %taps_ref.1, f32[1,512]{1,0:T(1,128)} %bitcast.1, ...), custom_call_target="tpu_custom_call" | custom-call | tf_op jit(solution)/shard_map/pallas_call | solution.py:438
  72.0 1.9 %copy.14 = bf16[512,512]{1,0:T(8,128)(2,1)} copy(bf16[512,512]{1,0:T(8,128)(2,1)} %shard_map.118) | data formatting | bytes 1048576

commit v7 on v6

--- a/solution.py
+++ b/solution.py
@@ -62,12 +62,12 @@
 def kernel(
     q_hbm, k_hbm, v_hbm, h_hbm, w_hbm, taps_ref, skip_ref,
     first_hbm, twist_hbm, second_hbm, second_back_hbm, first_back_hbm,
-    out_ref,
+    out_hbm,
     q_in, k_in, v_in, h_in, w_all, first, twist, second, second_back, first_back,
     rim, wide_k, wide_v, wide_q, turned_h, turned_x, mixed, queries,
     h_send, h_recv, x_send, x_recv, flat, spectra, y_flat, y_send, y_recv, back,
-    gated, far_send, far_recv, near_send, near_recv,
-    load_sem, rim_sems, w_load_sem, w_sems, h_sems, x_sems, y_sems, gated_sems, far_sems, near_sems,
+    gated, far_send, far_recv, near_send, near_recv, result,
+    load_sem, out_sem, rim_sems, w_load_sem, w_sems, h_sems, x_sems, y_sems, gated_sems, far_sems, near_sems,
 ):
     me_dp, me = lax.axis_index("dp"), lax.axis_index("ctx")
     chip, core = me_dp // 2, me_dp % 2
@@ -295,23 +295,27 @@
             invert(x_spec, step)
             x_spec = later
 
+    def piece(device, half):
+        rows = pl.ds(pl.multiple_of(device * CUTS * CHUNK + half * 16, 16), 16)
+        return y_flat[rows, :].astype(BF16)
+
+    def keep(chunk, half):
         @pl.loop(0, PARTS)
         def _(device):
-            rows = pl.ds(pl.multiple_of(device * CUTS * CHUNK, CUTS * CHUNK), CUTS * CHUNK)
-            value = y_flat[rows, :].astype(BF16)
-            for half in range(2):
-                y_send[chunk, half, device] = value[half * 16 : (half + 1) * 16]
+            y_send[chunk, half, device] = piece(device, half)
 
     def send_back(chunk, half):
         @pl.loop(0, PARTS - 1)
         def _(step):
             to = partner(step)
+            if half == 0:
+                y_send[chunk, half, to] = piece(to, half)
             remote(
                 y_send.at[chunk, half, to], y_recv.at[chunk, half, me], y_sems, (chunk, half),
                 (me_dp, to),
             ).start()
 
-        y_recv[chunk, half, me] = y_send[chunk, half, me]
+        y_recv[chunk, half, me] = y_send[chunk, half, me] if half else piece(me, half)
         some = pl.ds(0, PARTS - 1)
         return remote(
             y_send.at[chunk, half, some], y_recv.at[chunk, half, some], y_sems, (chunk, half),
@@ -328,9 +332,11 @@
     x_all[1] = send_mixed(1)
     convolve(0)
     y_all[0, 0] = send_back(0, 0)
+    keep(0, 1)
     filter_spectra(1)
     convolve(1)
     y_all[1, 0] = send_back(1, 0)
+    keep(1, 1)
 
     def gate(chunk, half):
         y_all[chunk, half].wait_recv()
@@ -397,7 +403,12 @@
             for way in range(2):
                 near[half, way, strip].wait_recv()
                 value = value + near_recv[half, way, strip].astype(F32)
-            out_ref[half * HALF : (half + 1) * HALF, strip * STRIP : (strip + 1) * STRIP] = value.astype(BF16)
+            result[half, :, strip * STRIP : (strip + 1) * STRIP] = value.astype(BF16)
+        copy = pltpu.make_async_copy(
+            result.at[half], out_hbm.at[pl.ds(half * HALF, HALF)], out_sem.at[half]
+        )
+        copy.start()
+        return copy
 
     rims[0].wait()
     arrive(0, wide_q)
@@ -418,9 +429,10 @@
     send_near(0, True)
     send_near(1, False)
     send_near(1, True)
-    finish(0)
-    finish(1)
-
+    stored = [finish(0), finish(1)]
+
+    for copy in stored:
+        copy.wait()
     y_all[0, 0].wait_send()
     for copy in [h_all[1], x_all[1], y_all[0, 1], y_all[1, 1], *far.values(), *near.values()]:
         copy.wait_send()
@@ -439,7 +451,7 @@
         kernel,
         out_shape=jax.ShapeDtypeStruct((ROWS, COLUMNS), BF16),
         in_specs=[anywhere] * 5 + [local] * 2 + [anywhere] * 5,
-        out_specs=local,
+        out_specs=anywhere,
         scratch_shapes=[
             *[pltpu.VMEM(stream, BF16)] * 4,
             pltpu.VMEM((2, CHIPS, CHANNELS, COLUMNS), BF16),
@@ -458,7 +470,9 @@
             pltpu.VMEM((2, ROWS, CHANNELS), BF16),
             *[pltpu.VMEM((2, 2, HALF, STRIP), BF16)] * 2,
             *[pltpu.VMEM((2, 2, 2, HALF, STRIP), BF16)] * 2,
+            pltpu.VMEM((2, HALF, COLUMNS), BF16),
             dma((9,)),
+            dma((2,)),
             dma((2, 3)),
             dma((CHIPS,)),
             dma((2, CHIPS)),

time: 74 us -> 73.8 us (level)
  no operation moved by 1% of the time
where the time goes in v7:
time: 73.8 us; the launch traced here: 73.6 us
  Pallas kernels  71.7 us (97%)
  local copies, waits for them, and re-layouts  1.87 us (3%)
    pallas_call x1, Pallas kernels, body(): pl.pallas_call(kernel, out_shape=jax.ShapeDtypeStruct((ROWS, COLUMNS), BF...  71.7 us
    unnamed x1, local copies, waits for them, and re-layouts  1.87 us

profile of v7, /device:TPU:1, one launch (start us, length us, event | category | flops | bytes accessed | tf_op | source)
XLA Modules:
  0.0 73.6 jit_solution(15409262885904982383)
XLA Ops:
  0.0 71.7 %shard_map.118 = bf16[512,512]{1,0:T(8,128)(2,1)} custom-call(bf16[512,512]{1,0:T(8,128)(2,1)} %q_hbm.1, bf16[512,512]{1,0:T(8,128)(2,1)} %k_hbm.1, bf16[512,512]{1,0:T(8,128)(2,1)} %v_hbm.1, bf16[512,512]{1,0:T(8,128)(2,1)} %h_hbm.1, bf16[512,4096]{1,0:T(8,128)(2,1)} %w_hbm.1, f32[3,3,512]{2,1,0:T(4,128)} %taps_ref.1, f32[1,512]{1,0:T(1,128)} %bitcast.1, ...), custom_call_target="tpu_custom_call" | custom-call | tf_op jit(solution)/shard_map/pallas_call | solution.py:450
  71.7 1.9 %copy.14 = bf16[512,512]{1,0:T(8,128)(2,1)} copy(bf16[512,512]{1,0:T(8,128)(2,1)} %shard_map.118) | data formatting | bytes 1048576

commit v8 on v7

--- a/solution.py
+++ b/solution.py
@@ -416,8 +416,8 @@
     exchanged = [gate(0, 0)]
     y_all[1, 0].wait_send()
     y_all[0, 1] = send_back(0, 1)
+    exchanged.append(gate(1, 0))
     y_all[1, 1] = send_back(1, 1)
-    exchanged.append(gate(1, 0))
     for copy in w_loads + w_sent + exchanged:
         copy.wait()
     send_far(0)

time: 73.8 us -> 75.1 us (1.018)
  Pallas kernels: 71.7 us -> 73.1 us
    pallas_call x1, Pallas kernels: 71.7 us -> 73.1 us  [body(): pl.pallas_call(kernel, out_shape=jax.ShapeDtypeStruct((ROWS, COLUMNS), BF...]
where the time goes in v8:
time: 75.1 us; the launch traced here: 74.9 us
  Pallas kernels  73.1 us (97%)
  local copies, waits for them, and re-layouts  1.87 us (2%)
    pallas_call x1, Pallas kernels, body(): pl.pallas_call(kernel, out_shape=jax.ShapeDtypeStruct((ROWS, COLUMNS), BF...  73.1 us
    unnamed x1, local copies, waits for them, and re-layouts  1.87 us

profile of v8, /device:TPU:1, one launch (start us, length us, event | category | flops | bytes accessed | tf_op | source)
XLA Modules:
  0.0 74.9 jit_solution(11427955313617302086)
XLA Ops:
  0.0 73.1 %shard_map.118 = bf16[512,512]{1,0:T(8,128)(2,1)} custom-call(bf16[512,512]{1,0:T(8,128)(2,1)} %q_hbm.1, bf16[512,512]{1,0:T(8,128)(2,1)} %k_hbm.1, bf16[512,512]{1,0:T(8,128)(2,1)} %v_hbm.1, bf16[512,512]{1,0:T(8,128)(2,1)} %h_hbm.1, bf16[512,4096]{1,0:T(8,128)(2,1)} %w_hbm.1, f32[3,3,512]{2,1,0:T(4,128)} %taps_ref.1, f32[1,512]{1,0:T(1,128)} %bitcast.1, ...), custom_call_target="tpu_custom_call" | custom-call | tf_op jit(solution)/shard_map/pallas_call | solution.py:450
  73.1 1.9 %copy.14 = bf16[512,512]{1,0:T(8,128)(2,1)} copy(bf16[512,512]{1,0:T(8,128)(2,1)} %shard_map.118) | data formatting | bytes 1048576
